TPU v7x, 32 devices: a whole 2x2x4 slice. The times are simulated.
32 devices in a mesh: seq: 16 (over z, y, core), mp: 2 (over x).
Axes of the slice: x: 2, y: 2, z: 4, core: 2. Of those that a mesh axis runs over, the one named last changes fastest.
Arguments:
- tokens: bfloat16 [16384, 4096], P('seq', 'mp'), may hold values from -6 to 6
- segment_ids: int32 [16384], P('seq'), may hold values from 0 to 3, never falling along the last dimension, each value on 1 to 8192 neighbouring positions
- w_x: bfloat16 [4096, 4096], P(None, 'mp'), may hold values from -0.09375 to 0.09375
- w_z: bfloat16 [4096, 4096], P(None, 'mp'), may hold values from -0.09375 to 0.09375
- w_bc: bfloat16 [4096, 256], replicated, may hold values from -0.09375 to 0.09375
- w_dt: bfloat16 [4096, 32], P(None, 'mp'), may hold values from -0.09375 to 0.09375
- dt_bias: float32 [32], P('mp'), may hold values from -1 to 1
- rates: float32 [32], P('mp'), may hold values from 3.0517578e-05 to 0.05
- conv_x: float32 [3, 4096], P(None, 'mp'), may hold values from -3 to 3
- conv_bc: float32 [3, 256], replicated, may hold values from -3 to 3
- norm_gain: float32 [4096], P('mp'), may hold values from 0.5 to 1.5
Outputs:
- encoded: bfloat16 [16384, 4096], P('seq', 'mp')
Inputs may be any that keep to these rules, and one draw needn't show every extreme that they name: `segment_ids`: document numbers never fall along the slab and start at 0; each document holds 1 to 8192 tokens, and one holds exactly 8192.
All inputs are finite; a program needn't handle non-finite values.
Results may differ from a plain program's by a relative error of at most 0.009.
Values may be sent and summed in bfloat16 or wider, within the bound.
A program may use at most 192 MiB of HBM per device.

v0:
```python
import functools

import jax
import jax.numpy as jnp
from jax import lax
from jax.experimental import pallas as pl
from jax.experimental.pallas import tpu as pltpu
from jax.sharding import PartitionSpec as P

BLOCK = 256
LANES = 128
GROUP = 4
LOG2E = 1.4426950408889634
MESH = pl.DeviceIdType.MESH
VMEM_LIMIT = 60 * 1024 * 1024
F32 = jnp.float32
BF16 = jnp.bfloat16


def silu(v):
    return v / (1.0 + jnp.exp(-v))


def filtered(x, prev, nxt, m_prev, m_next, taps):
    rows = lax.broadcasted_iota(jnp.int32, x.shape, 0)
    last = x.shape[0] - 1
    before = jnp.where(rows == 0, prev, pltpu.roll(x, 1, axis=0)) * m_prev
    after = jnp.where(rows == last, nxt, pltpu.roll(x, last, axis=0)) * m_next
    return silu(taps[0:1] * before + taps[1:2] * x + taps[2:3] * after).astype(BF16)


def local_kernel(
    heads, x_ref, bc_ref, prev_ref, next_ref, raw_ref, bias_ref, rate_ref, aux_ref, seg_ref,
    taps_ref, taps_bc_ref,
    inside_ref, c_ref, opf_ref, opb_ref, sf_ref, sb_ref, dec_ref, tot_ref, totdec_ref,
    accf, accb, run,
):
    step = pl.program_id(0)
    inner = heads * LANES

    @pl.when(step == 0)
    def _():
        accf[...] = jnp.zeros_like(accf)
        accb[...] = jnp.zeros_like(accb)
        run[...] = jnp.ones_like(run)

    aux = aux_ref[...]
    seg_col, m_prev, m_next = aux[:, 0:1], aux[:, 1:2], aux[:, 2:3]
    from_prev, from_next = aux[:, 3:4], aux[:, 4:5]
    with_first, with_last = aux[:, 5:6], aux[:, 6:7]

    raw = raw_ref[...] + bias_ref[...]
    dt = jnp.maximum(raw, 0.0) + jnp.log1p(jnp.exp(-jnp.abs(raw)))
    drop = dt * (rate_ref[...] * -LOG2E)
    row_at = lax.broadcasted_iota(jnp.int32, (BLOCK, BLOCK), 0)
    col_at = lax.broadcasted_iota(jnp.int32, (BLOCK, BLOCK), 1)
    lower = col_at <= row_at
    incl = jnp.dot(lower.astype(F32), drop, precision=lax.Precision.HIGHEST, preferred_element_type=F32)
    excl = jnp.dot((col_at < row_at).astype(F32), drop, precision=lax.Precision.HIGHEST, preferred_element_type=F32)
    total = incl[BLOCK - 1:BLOCK]
    opf_ref[...] = jnp.exp2(incl) * from_prev
    opb_ref[...] = jnp.exp2(total - excl) * from_next
    tail_f = jnp.exp2(total - incl) * with_last * dt
    tail_b = jnp.exp2(excl) * with_first * dt
    whole = jnp.exp2(total)
    dec_f = whole * from_prev[BLOCK - 1:BLOCK]
    dec_b = whole * from_next[0:1]
    dec_ref[0] = jnp.concatenate([dec_f, dec_b, jnp.zeros((6, LANES), F32)], axis=0)
    incl_t, excl_t, dt_t = incl.T, excl.T, dt.T

    bcs = filtered(
        bc_ref[...].astype(F32), prev_ref[0][:, inner:], next_ref[0][:, inner:], m_prev, m_next,
        taps_bc_ref[...],
    )
    c_vecs = bcs[:, LANES:]
    c_ref[...] = c_vecs
    b_t = bcs[:, :LANES].astype(F32).T.astype(BF16)
    scores = jnp.dot(c_vecs, b_t, preferred_element_type=F32)
    scores = jnp.where(seg_col == seg_ref[0], scores, 0.0)

    run_b = run[...]
    for h in range(heads):
        cols = slice(h * LANES, (h + 1) * LANES)
        xs = filtered(
            x_ref[:, cols].astype(F32), prev_ref[0][:, cols], next_ref[0][:, cols], m_prev, m_next,
            taps_ref[:, cols],
        )
        one = slice(h, h + 1)
        gap = jnp.where(lower, incl[:, one] - incl_t[one], excl_t[one] - excl[:, one])
        weights = (scores * jnp.exp2(gap) * dt_t[one]).astype(BF16)
        inside_ref[:, cols] = jnp.dot(weights, xs, preferred_element_type=F32)
        wide = xs.astype(F32)
        fresh_f = jnp.dot(b_t, (wide * tail_f[:, one]).astype(BF16), preferred_element_type=F32)
        fresh_b = jnp.dot(b_t, (wide * tail_b[:, one]).astype(BF16), preferred_element_type=F32)
        sf_ref[0, :, cols] = fresh_f
        sb_ref[0, :, cols] = fresh_b
        accf[:, cols] = accf[:, cols] * dec_f[:, one] + fresh_f
        accb[:, cols] = accb[:, cols] + run_b[1:2, one] * fresh_b
    run[...] = run_b * dec_ref[0]

    @pl.when(step == pl.num_programs(0) - 1)
    def _():
        part = LANES // GROUP
        for q in range(GROUP):
            tot_ref[q, 0] = accf[q * part:(q + 1) * part, :].astype(BF16)
            tot_ref[q, 1] = accb[q * part:(q + 1) * part, :].astype(BF16)
        totdec_ref[...] = run_b * dec_ref[0]


def local_part(xp, bc, prev, nxt, raw, bias, rate, aux, seg_rows, taps, taps_bc, heads):
    tok, inner = xp.shape
    blocks = tok // BLOCK
    part = LANES // GROUP
    row = lambda b: (b, 0)
    lead = lambda b: (b, 0, 0)
    fixed = lambda b: (0, 0)
    flops = tok * heads * (2 * BLOCK * LANES + 4 * LANES * LANES)
    return pl.pallas_call(
        functools.partial(local_kernel, heads),
        grid=(blocks,),
        in_specs=[
            pl.BlockSpec((BLOCK, inner), row),
            pl.BlockSpec((BLOCK, 2 * LANES), row),
            pl.BlockSpec((1, 1, inner + 2 * LANES), lead),
            pl.BlockSpec((1, 1, inner + 2 * LANES), lead),
            pl.BlockSpec((BLOCK, LANES), row),
            pl.BlockSpec((1, LANES), fixed),
            pl.BlockSpec((1, LANES), fixed),
            pl.BlockSpec((BLOCK, 8), row),
            pl.BlockSpec((1, 1, BLOCK), lead),
            pl.BlockSpec((3, inner), fixed),
            pl.BlockSpec((3, 2 * LANES), fixed),
        ],
        out_specs=[
            pl.BlockSpec((BLOCK, inner), row),
            pl.BlockSpec((BLOCK, LANES), row),
            pl.BlockSpec((BLOCK, LANES), row),
            pl.BlockSpec((BLOCK, LANES), row),
            pl.BlockSpec((1, LANES, inner), lead),
            pl.BlockSpec((1, LANES, inner), lead),
            pl.BlockSpec((1, 8, LANES), lead),
            pl.BlockSpec((GROUP, 2, part, inner), lambda b: (0, 0, 0, 0)),
            pl.BlockSpec((8, LANES), fixed),
        ],
        out_shape=[
            jax.ShapeDtypeStruct((tok, inner), F32),
            jax.ShapeDtypeStruct((tok, LANES), BF16),
            jax.ShapeDtypeStruct((tok, LANES), F32),
            jax.ShapeDtypeStruct((tok, LANES), F32),
            jax.ShapeDtypeStruct((blocks, LANES, inner), F32),
            jax.ShapeDtypeStruct((blocks, LANES, inner), F32),
            jax.ShapeDtypeStruct((blocks, 8, LANES), F32),
            jax.ShapeDtypeStruct((GROUP, 2, part, inner), BF16),
            jax.ShapeDtypeStruct((8, LANES), F32),
        ],
        scratch_shapes=[
            pltpu.VMEM((LANES, inner), F32),
            pltpu.VMEM((LANES, inner), F32),
            pltpu.VMEM((8, LANES), F32),
        ],
        compiler_params=pltpu.CompilerParams(
            dimension_semantics=("arbitrary",), vmem_limit_bytes=VMEM_LIMIT
        ),
        cost_estimate=pl.CostEstimate(
            flops=flops, bytes_accessed=tok * inner * 6 + 4 * inner * LANES * 8,
            transcendentals=tok * BLOCK * heads,
        ),
        name="local_part",
    )(xp, bc, prev, nxt, raw, bias, rate, aux, seg_rows, taps, taps_bc)


def spread(row, heads):
    return jnp.concatenate(
        [jnp.broadcast_to(row[:, h:h + 1], (1, LANES)) for h in range(heads)], axis=1
    )


def product(terms):
    out = terms[0]
    for term in terms[1:]:
        out = out * term
    return out


def exchange_kernel(
    heads, zs, tot_ref, dec_ref, ent_ref,
    near, near_dec, sums, sums_dec, far_f, far_b, far_dec, back, landed,
    near_s, near_r, dec_s, dec_r, f_s, f_r, b_s, b_r, fd_s, fd_r, back_s, back_r,
):
    me = lax.axis_index("seq")
    i = lax.rem(me, GROUP)
    z = lax.div(me, GROUP)
    low, high = lax.rem(i, 2), lax.div(i, 2)
    members = [i]
    for r in range(1, GROUP):
        other_low = 1 - low if r % 2 else low
        other_high = 1 - high if r // 2 else high
        members.append(other_high * 2 + other_low)
    far_dec[...] = jnp.ones_like(far_dec)
    far_f[...] = jnp.zeros_like(far_f)
    far_b[...] = jnp.zeros_like(far_b)

    barrier = pltpu.get_barrier_semaphore()
    for r in range(1, GROUP):
        pl.semaphore_signal(
            barrier, inc=1, device_id={"seq": z * GROUP + members[r]}, device_id_type=MESH
        )
    for d in range(1, zs):
        pl.semaphore_signal(
            barrier, inc=1, device_id={"seq": lax.rem(z + d, zs) * GROUP + i}, device_id_type=MESH
        )
    pl.semaphore_wait(barrier, GROUP - 1 + zs - 1)

    def send(src, dst, ssem, rsem, to):
        return pltpu.make_async_remote_copy(
            src_ref=src, dst_ref=dst, send_sem=ssem, recv_sem=rsem,
            device_id={"seq": to}, device_id_type=MESH,
        )

    firsts = []
    for r in range(1, GROUP):
        to = z * GROUP + members[r]
        firsts.append(send(dec_ref, near_dec.at[r], dec_s.at[r], dec_r.at[r], to))
        firsts.append(send(tot_ref.at[members[r]], near.at[r], near_s.at[r], near_r.at[r], to))
    for copy in firsts:
        copy.start()
    for copy in firsts:
        copy.wait()

    decs = [dec_ref[...]] + [near_dec[r] for r in range(1, GROUP)]

    def state(r, way):
        value = tot_ref[i, way] if r == 0 else near[r, way]
        return value.astype(F32)

    def between(r, s, way):
        terms = []
        for k in range(GROUP):
            if way == 0:
                inside = (members[k] > members[r]) & (members[k] < members[s])
            else:
                inside = (members[k] < members[r]) & (members[k] > members[s])
            terms.append(jnp.where(inside, decs[k][way:way + 1], 1.0))
        return product(terms)

    def beyond(r, way):
        terms = []
        for k in range(GROUP):
            if way == 0:
                inside = members[k] > members[r]
            else:
                inside = members[k] < members[r]
            terms.append(jnp.where(inside, decs[k][way:way + 1], 1.0))
        return product(terms)

    for way in range(2):
        total = jnp.zeros(sums.shape[1:], F32)
        for r in range(GROUP):
            total = total + spread(beyond(r, way), heads) * state(r, way)
        sums[way] = total.astype(BF16)
    sums_dec[...] = product(decs)

    for d in range(1, zs):
        up = (z + d) * GROUP + i
        down = (z - d) * GROUP + i

        @pl.when(z + d < zs)
        def _():
            send(sums_dec, far_dec.at[0, d], fd_s.at[0, d], fd_r.at[0, d], up).start()
            send(sums.at[0], far_f.at[d], f_s.at[d], f_r.at[d], up).start()

        @pl.when(z - d >= 0)
        def _():
            send(sums_dec, far_dec.at[1, d], fd_s.at[1, d], fd_r.at[1, d], down).start()
            send(sums.at[1], far_b.at[d], b_s.at[d], b_r.at[d], down).start()

    for d in range(1, zs):
        up = (z + d) * GROUP + i
        down = (z - d) * GROUP + i

        @pl.when(z - d >= 0)
        def _():
            send(sums_dec, far_dec.at[0, d], fd_s.at[0, d], fd_r.at[0, d], down).wait_recv()
            send(sums.at[0], far_f.at[d], f_s.at[d], f_r.at[d], down).wait_recv()

        @pl.when(z + d < zs)
        def _():
            send(sums_dec, far_dec.at[1, d], fd_s.at[1, d], fd_r.at[1, d], up).wait_recv()
            send(sums.at[1], far_b.at[d], b_s.at[d], b_r.at[d], up).wait_recv()

    for way in range(2):
        far = far_b if way else far_f
        entering = jnp.zeros(sums.shape[1:], F32)
        weight = jnp.ones((1, LANES), F32)
        for d in range(1, zs):
            entering = entering + spread(weight, heads) * far[d].astype(F32)
            weight = weight * far_dec[way, d][way:way + 1]
        for s in range(GROUP):
            terms = []
            for k in range(GROUP):
                if way == 0:
                    earlier = members[k] < members[s]
                else:
                    earlier = members[k] > members[s]
                terms.append(jnp.where(earlier, decs[k][way:way + 1], 1.0))
            value = spread(product(terms), heads) * entering
            for r in range(GROUP):
                if r != s:
                    if way == 0:
                        earlier = members[r] < members[s]
                    else:
                        earlier = members[r] > members[s]
                    weight = jnp.where(earlier, between(r, s, way), 0.0)
                    value = value + spread(weight, heads) * state(r, way)
            back[s, way] = value.astype(BF16)

    lasts = []
    for r in range(1, GROUP):
        to = z * GROUP + members[r]
        lasts.append(send(back.at[r], landed.at[r], back_s.at[r], back_r.at[r], to))
    for copy in lasts:
        copy.start()
    ent_ref[i] = back[0]
    for r in range(1, GROUP):
        lasts[r - 1].wait()
        ent_ref[members[r]] = landed[r]

    for d in range(1, zs):
        up = (z + d) * GROUP + i
        down = (z - d) * GROUP + i

        @pl.when(z + d < zs)
        def _():
            send(sums_dec, far_dec.at[0, d], fd_s.at[0, d], fd_r.at[0, d], up).wait_send()
            send(sums.at[0], far_f.at[d], f_s.at[d], f_r.at[d], up).wait_send()

        @pl.when(z - d >= 0)
        def _():
            send(sums_dec, far_dec.at[1, d], fd_s.at[1, d], fd_r.at[1, d], down).wait_send()
            send(sums.at[1], far_b.at[d], b_s.at[d], b_r.at[d], down).wait_send()


def exchange(tot, totdec, heads):
    zs = lax.axis_size("seq") // GROUP
    _, _, part, inner = tot.shape
    dma = pltpu.SemaphoreType.DMA
    vmem = pl.BlockSpec(memory_space=pltpu.VMEM)
    return pl.pallas_call(
        functools.partial(exchange_kernel, heads, zs),
        in_specs=[vmem, vmem],
        out_specs=vmem,
        out_shape=jax.ShapeDtypeStruct(tot.shape, BF16),
        scratch_shapes=[
            pltpu.VMEM((GROUP, 2, part, inner), BF16),
            pltpu.VMEM((GROUP, 8, LANES), F32),
            pltpu.VMEM((2, part, inner), BF16),
            pltpu.VMEM((8, LANES), F32),
            pltpu.VMEM((zs, part, inner), BF16),
            pltpu.VMEM((zs, part, inner), BF16),
            pltpu.VMEM((2, zs, 8, LANES), F32),
            pltpu.VMEM((GROUP, 2, part, inner), BF16),
            pltpu.VMEM((GROUP, 2, part, inner), BF16),
            dma((GROUP,)), dma((GROUP,)), dma((GROUP,)), dma((GROUP,)),
            dma((zs,)), dma((zs,)), dma((zs,)), dma((zs,)),
            dma((2, zs)), dma((2, zs)),
            dma((GROUP,)), dma((GROUP,)),
        ],
        compiler_params=pltpu.CompilerParams(
            collective_id=1, has_side_effects=True, vmem_limit_bytes=VMEM_LIMIT
        ),
        cost_estimate=pl.CostEstimate(
            flops=tot.size * 20, bytes_accessed=tot.size * 8, transcendentals=0
        ),
        name="exchange_states",
    )(tot, totdec)


def finish_kernel(
    heads, inside_ref, c_ref, opf_ref, opb_ref, gate_ref, sf_ref, sb_ref, dec_ref, decs_ref,
    ent_ref, out_ref, sq_ref, hf, hb,
):
    step = pl.program_id(0)
    blocks = hb.shape[0]
    part = LANES // GROUP

    @pl.when(step == 0)
    def _():
        for q in range(GROUP):
            hf[q * part:(q + 1) * part, :] = ent_ref[q, 0].astype(F32)
        for h in range(heads):
            cols = slice(h * LANES, (h + 1) * LANES)
            now = jnp.concatenate([ent_ref[q, 1, :, cols] for q in range(GROUP)], axis=0).astype(F32)
            for b in range(blocks - 1, -1, -1):
                hb[b, :, cols] = now.astype(BF16)
                if b:
                    now = now * decs_ref[b, 1:2, h:h + 1] + sb_ref[b, :, cols]

    c_vecs = c_ref[...]
    opf, opb = opf_ref[...], opb_ref[...]
    squares = jnp.zeros((BLOCK, LANES), F32)
    for h in range(heads):
        cols = slice(h * LANES, (h + 1) * LANES)
        one = slice(h, h + 1)
        state = hf[:, cols]
        got_f = jnp.dot(c_vecs, state.astype(BF16), preferred_element_type=F32)
        got_b = jnp.dot(c_vecs, hb[step, :, cols], preferred_element_type=F32)
        hf[:, cols] = state * dec_ref[0, 0:1, one] + sf_ref[0, :, cols]
        mixed = inside_ref[:, cols] + got_f * opf[:, one] + got_b * opb[:, one]
        gated = mixed * silu(gate_ref[:, cols].astype(F32))
        squares = squares + gated * gated
        out_ref[:, cols] = gated
    sq_ref[...] = jnp.sum(squares, axis=1, keepdims=True)


def finish(inside, c_vecs, opf, opb, gate, sf, sb, dec, ent, heads):
    tok, inner = inside.shape
    blocks = tok // BLOCK
    part = LANES // GROUP
    row = lambda b: (b, 0)
    lead = lambda b: (b, 0, 0)
    whole = lambda b: (0, 0, 0)
    return pl.pallas_call(
        functools.partial(finish_kernel, heads),
        grid=(blocks,),
        in_specs=[
            pl.BlockSpec((BLOCK, inner), row),
            pl.BlockSpec((BLOCK, LANES), row),
            pl.BlockSpec((BLOCK, LANES), row),
            pl.BlockSpec((BLOCK, LANES), row),
            pl.BlockSpec((BLOCK, inner), row),
            pl.BlockSpec((1, LANES, inner), lead),
            pl.BlockSpec((blocks, LANES, inner), whole),
            pl.BlockSpec((1, 8, LANES), lead),
            pl.BlockSpec((blocks, 8, LANES), whole),
            pl.BlockSpec((GROUP, 2, part, inner), lambda b: (0, 0, 0, 0)),
        ],
        out_specs=[pl.BlockSpec((BLOCK, inner), row), pl.BlockSpec((BLOCK, 1), row)],
        out_shape=[
            jax.ShapeDtypeStruct((tok, inner), F32),
            jax.ShapeDtypeStruct((tok, 1), F32),
        ],
        scratch_shapes=[
            pltpu.VMEM((LANES, inner), F32),
            pltpu.VMEM((blocks, LANES, inner), BF16),
        ],
        compiler_params=pltpu.CompilerParams(
            dimension_semantics=("arbitrary",), vmem_limit_bytes=VMEM_LIMIT
        ),
        cost_estimate=pl.CostEstimate(
            flops=tok * inner * LANES * 4, bytes_accessed=tok * inner * 10, transcendentals=tok * inner
        ),
        name="finish",
    )(inside, c_vecs, opf, opb, gate, sf, sb, dec, dec, ent)


def neighbours(rows):
    count = lax.axis_size("seq")
    from_left = lax.ppermute(rows[-1:], "seq", [(i, i + 1) for i in range(count - 1)])
    from_right = lax.ppermute(rows[:1], "seq", [(i + 1, i) for i in range(count - 1)])
    return from_left, from_right


def shards(tokens, segment_ids, w_x, w_z, w_bc, w_dt, dt_bias, rates, conv_x, conv_bc, norm_gain):
    tok = tokens.shape[0]
    inner = w_x.shape[1]
    heads = w_dt.shape[1]
    mp_count = lax.axis_size("mp")
    seq_count = lax.axis_size("seq")
    position = lax.axis_index("seq")
    blocks = tok // BLOCK

    seg = segment_ids.astype(F32)
    seg_left, seg_right = neighbours(seg)
    seg_left = jnp.where(position > 0, seg_left, -1.0)
    seg_right = jnp.where(position < seq_count - 1, seg_right, -1.0)
    before = jnp.concatenate([seg_left, seg[:-1]])
    after = jnp.concatenate([seg[1:], seg_right])
    by_block = lambda v: jnp.repeat(v, BLOCK)
    aux = jnp.stack(
        [
            seg,
            (seg == before).astype(F32),
            (seg == after).astype(F32),
            (seg == by_block(before[::BLOCK])).astype(F32),
            (seg == by_block(after[BLOCK - 1::BLOCK])).astype(F32),
            (seg == by_block(seg[::BLOCK])).astype(F32),
            (seg == by_block(seg[BLOCK - 1::BLOCK])).astype(F32),
            seg,
        ],
        axis=1,
    )
    seg_rows = seg.reshape(blocks, 1, BLOCK)
    w_small = jnp.concatenate([w_bc, jnp.pad(w_dt, ((0, 0), (0, LANES - heads)))], axis=1)
    bias = jnp.pad(dt_bias, (0, LANES - heads))[None]
    rate = jnp.pad(rates, (0, LANES - heads))[None]

    piece = lax.all_gather(tokens, "mp", axis=1, tiled=True)
    small = jnp.dot(piece, w_small, preferred_element_type=F32)
    bc = small[:, :2 * LANES].astype(BF16)
    raw = small[:, 2 * LANES:]
    xp = jnp.dot(piece, w_x, preferred_element_type=F32).astype(BF16)
    gate = jnp.dot(piece, w_z, preferred_element_type=F32).astype(BF16)

    firsts = jnp.concatenate([xp[::BLOCK], bc[::BLOCK]], axis=1).astype(F32)
    lasts = jnp.concatenate([xp[BLOCK - 1::BLOCK], bc[BLOCK - 1::BLOCK]], axis=1).astype(F32)
    from_left = lax.ppermute(lasts[-1:], "seq", [(i, i + 1) for i in range(seq_count - 1)])
    from_right = lax.ppermute(firsts[:1], "seq", [(i + 1, i) for i in range(seq_count - 1)])
    prev = jnp.concatenate([from_left, lasts[:-1]], axis=0)[:, None]
    nxt = jnp.concatenate([firsts[1:], from_right], axis=0)[:, None]

    inside, c_vecs, opf, opb, sf, sb, dec, tot, totdec = local_part(
        xp, bc, prev, nxt, raw, bias, rate, aux, seg_rows, conv_x, conv_bc, heads
    )
    ent = exchange(tot, totdec, heads)
    gated, sq = finish(inside, c_vecs, opf, opb, gate, sf, sb, dec, ent, heads)
    squares = lax.psum(sq, "mp")
    scale = lax.rsqrt(squares / (inner * mp_count) + 1e-05)
    return (gated * scale * norm_gain).astype(BF16)


def solution(mesh):
    placed = (
        P("seq", "mp"),
        P("seq"),
        P(None, "mp"),
        P(None, "mp"),
        P(),
        P(None, "mp"),
        P("mp"),
        P("mp"),
        P(None, "mp"),
        P(),
        P("mp"),
    )
    return jax.shard_map(
        shards, mesh=mesh, in_specs=placed, out_specs=P("seq", "mp"), check_vma=False
    )
```

profile of v0, /device:TPU:0, one launch (start us, length us, event | category | flops | bytes accessed | tf_op | source)
XLA Modules:
  0.0 298.6 jit_solution(15279546666128000140)
XLA Ops:
  6.5 0.0 all-gather.2.cloned.1.call-start
  6.5 0.7 all-gather.2.cloned.1.call-update
  7.3 0.7 convert_element_type.33
  7.9 0.0 copy-start.1
  8.0 0.7 fusion.16
  8.6 1.3 collective-permute-start.3
  9.9 3.5 %collective-permute-start.2 = (f32[1]{0:T(128)}, f32[1]{0:T(128)}, u32[]{:S(2)}, u32[]{:S(2)}) collective-permute-start(f32[1]{0:T(128)} %get-tuple-element.37), channel_id=1, source_target_pairs={{0,2},{2,4},{4,6},{6,8},{8,10},{10,12},{12,14},{14,16},{16,18},{18... | collective-permute-start | bytes 20 | tf_op jit(solution)/shard_map/ppermute | solution.py:458
  13.4 0.1 slice.72
  13.5 0.1 slice.71
  13.6 0.1 broadcast_bitcast_fusion.1
  13.7 0.1 broadcast_bitcast_fusion
  13.8 1.4 copy.31
  15.2 1.2 pad_bitcast_fusion
  16.4 0.1 fusion.15
  16.5 0.0 collective-permute-done.3
  17.1 0.8 compare_convert_fusion.4
  17.9 0.1 slice.70
  18.0 0.1 broadcast_bitcast_fusion.2
  18.0 0.0 collective-permute-done.2
  18.6 0.8 compare_convert_fusion.5
  19.4 0.1 slice.69
  19.5 0.1 broadcast_bitcast_fusion.3
  19.6 0.7 compare_convert_fusion.3
  20.3 0.1 stack.56
  20.3 1.0 copy.29.aux_ref
  21.4 94.3 %all-gather.2.cloned.1.call-done = bf16[1024,4096]{1,0:T(8,128)(2,1)} async-done(((bf16[1024,2048]{1,0:T(8,128)(2,1)}), bf16[1024,4096]{1,0:T(8,128)(2,1)}) %all-gather.2.cloned.1.call-update) | async-done | bytes 8388624 | tf_op jit(solution)/shard_map/all_gather | solution.py:497
  115.7 7.6 %fusion.8 = f32[1024,384]{1,0:T(8,128)S(1)} fusion(bf16[1024,4096]{1,0:T(8,128)(2,1)} %all-gather.2.cloned.1.call-done, bf16[4096,16]{1,0:T(8,128)(2,1)S(1)} %copy.31, bf16[4096,256]{1,0:T(8,128)(2,1)} %param.15), kind=kOutput, calls=%fused_computation.11 | convolution fusion | flops 3230662656 | bytes 12189696 | tf_op jit(solution)/shard_map/dot_general | solution.py:498
  123.2 0.0 copy-done.1
  123.3 0.1 slice.77.bc_ref
  123.3 0.0 copy-start
  123.4 23.7 %convolution_convert_fusion.1.x_ref = bf16[1024,2048]{1,0:T(8,128)(2,1)} fusion(bf16[1024,4096]{1,0:T(8,128)(2,1)} %all-gather.2.cloned.1.call-done, bf16[4096,2048]{1,0:T(8,128)(2,1)} %param.13), kind=kOutput, calls=%fused_computation.4 | convolution fusion | flops 17181966336 | bytes 29360128 | tf_op jit(solution)/shard_map/dot_general | solution.py:501
  147.1 0.0 copy-done
  147.1 2.2 slice.60
  149.4 1.9 slice.56
  151.4 1.8 collective-permute-start
  153.1 23.7 %convolution_convert_fusion.gate_ref = bf16[1024,2048]{1,0:T(8,128)(2,1)} fusion(bf16[1024,4096]{1,0:T(8,128)(2,1)} %all-gather.2.cloned.1.call-done, bf16[4096,2048]{1,0:T(8,128)(2,1)} %param.14), kind=kOutput, calls=%fused_computation.3 | convolution fusion | flops 17181966336 | bytes 29360128 | tf_op jit(solution)/shard_map/dot_general | solution.py:502
  176.9 0.8 slice.75.raw_ref
  177.7 1.5 collective-permute-start.1
  179.2 0.0 collective-permute-done
  179.2 0.6 copy.28.prev_ref
  179.9 2.2 collective-permute-done.1
  182.1 0.6 broadcast_in_dim.29.next_ref
  182.7 20.2 %local_part.1 = (f32[1024,2048]{1,0:T(8,128)}, bf16[1024,128]{1,0:T(8,128)(2,1)}, f32[1024,128]{1,0:T(8,128)}, f32[1024,128]{1,0:T(8,128)}, f32[4,128,2048]{2,1,...) custom-call(bf16[1024,2048]{1,0:T(8,128)(2,1)} %convolution_convert_, ...), custom_call_target="tpu_custom_call" | custom-call | flops 2147483648 | bytes 20971520 | tf_op jit(solution)/shard_map/local_part/pallas_call | solution.py:118
  202.9 48.7 %exchange_states.1.ent_ref = bf16[4,2,32,2048]{3,2,1,0:T(8,128)(2,1)} custom-call(bf16[4,2,32,2048]{3,2,1,0:T(8,128)(2,1)} %get-tuple-element.23.tot_ref, f32[8,128]{1,0:T(8,128)} %get-tuple-element.24.dec_ref), custom_call_target="tpu_custom_call" | custom-call | flops 10485760 | bytes 4194304 | tf_op jit(solution)/shard_map/exchange_states/pallas_call | solution.py:348
  251.5 0.0 copy-start.2
  251.6 15.4 %finish.1 = (f32[1024,2048]{1,0:T(8,128)}, f32[1024,1]{1,0:T(8,128)}) custom-call(f32[1024,2048]{1,0:T(8,128)} %get-tuple-element.16.inside_ref, bf16[1024,128]{1,0:T(8,128)(2,1)} %get-tuple-element.17.c_ref, f32[1024,128]{1,0:T(8,128)} %get-tuple-element.18.opf_ref, f32[1024,128]{1,0:T(8,128)} %get-tuple-element.19.opb_ref, ...), custom_call_target="tpu_custom_call" | custom-call | flops 1073741824 | bytes 20971520 | tf_op jit(solution)/shard_map/finish/pallas_call | solution.py:422
  267.0 18.4 %psum.7 = f32[1024,1]{1,0:T(8,128)S(1)} all-reduce(f32[1024,1]{1,0:T(8,128)} %get-tuple-element.26), channel_id=1, replica_groups=mesh['seq'=16,'mp'=2] {'mp'}, use_global_device_ids=true, to_apply=%region_0.1 | all-reduce | flops 1024 | bytes 8192 | tf_op jit(solution)/shard_map/psum | solution.py:516
  285.4 0.2 rsqrt_reduce_fusion
  285.6 0.0 copy-done.2
  285.6 6.1 %multiply_convert_fusion = bf16[1024,2048]{1,0:T(8,128)(2,1)} fusion(f32[1024,2048]{1,0:T(8,128)} %get-tuple-element.25, f32[2048]{0:T(1024)S(1)} %copy-done.2, f32[1024]{0:T(1024)S(1)} %rsqrt_reduce_fusion), kind=kLoop, calls=%fused_computation | loop fusion | flops 6291456 | bytes 12595200 | tf_op jit(solution)/shard_map/convert_element_type | solution.py:518
  (13 shorter events, 0.2 us)
Async XLA Ops:
  6.5 109.1 %all-gather.2.cloned.1.call-start = ((), (), s32[]{:S(2)}) async-start(), calls=%async_computation | async-start | bytes 12582912 | tf_op jit(solution)/shard_map/all_gather | solution.py:497
  7.9 115.3 %copy-start.1 = (f32[1024]{0:T(1024)}, f32[1024]{0:T(1024)S(1)}, u32[]{:S(2)}) copy-start(f32[1024]{0:T(1024)S(1)} %convert_element_type.33) | copy-start | bytes 12292
  8.6 7.9 %collective-permute-start.3 = (f32[1]{0:T(128)}, f32[1]{0:T(128)}, u32[]{:S(2)}, u32[]{:S(2)}) collective-permute-start(f32[1]{0:T(128)} %get-tuple-element.36), channel_id=1, source_target_pairs={{2,0},{4,2},{6,4},{8,6},{10,8},{12,10},{14,12},{16,14},{18,16},{20... | collective-permute-start | bytes 20 | tf_op jit(solution)/shard_map/ppermute | solution.py:459
  9.9 8.2 %collective-permute-start.2 = (f32[1]{0:T(128)}, f32[1]{0:T(128)}, u32[]{:S(2)}, u32[]{:S(2)}) collective-permute-start(f32[1]{0:T(128)} %get-tuple-element.37), channel_id=1, source_target_pairs={{0,2},{2,4},{4,6},{6,8},{8,10},{10,12},{12,14},{14,16},{16,18},{18... | collective-permute-start | bytes 20 | tf_op jit(solution)/shard_map/ppermute | solution.py:458
  123.3 23.8 %copy-start = (bf16[1024,256]{1,0:T(8,128)(2,1)}, bf16[1024,256]{1,0:T(8,128)(2,1)S(1)}, u32[]{:S(2)}) copy-start(bf16[1024,256]{1,0:T(8,128)(2,1)S(1)} %slice.77.bc_ref) | copy-start | bytes 1572868
  151.4 27.8 %collective-permute-start = (f32[1,2304]{1,0:T(1,128)S(1)}, f32[1,2304]{1,0:T(1,128)S(1)}, u32[]{:S(2)}, u32[]{:S(2)}) collective-permute-start(f32[1,2304]{1,0:T(1,128)S(1)} %maximum_convert_fusion.2), channel_id=1, source_target_pairs={{0,2},{2,4},{4,6},{6,8},{8,10},{10,12},{12,14},{14,16},{16,18},{18... | collective-permute-start | bytes 27656 | tf_op jit(solution)/shard_map/ppermute | solution.py:506
  177.7 4.3 %collective-permute-start.1 = (f32[1,2304]{1,0:T(1,128)S(1)}, f32[1,2304]{1,0:T(1,128)S(1)}, u32[]{:S(2)}, u32[]{:S(2)}) collective-permute-start(f32[1,2304]{1,0:T(1,128)S(1)} %maximum_convert_fusion.1), channel_id=1, source_target_pairs={{2,0},{4,2},{6,4},{8,6},{10,8},{12,10},{14,12},{16,14},{18,16},{20... | collective-permute-start | bytes 27656 | tf_op jit(solution)/shard_map/ppermute | solution.py:507
  251.5 34.0 %copy-start.2 = (f32[2048]{0:T(1024)S(1)}, f32[2048]{0:T(1024)}, u32[]{:S(2)}) copy-start(f32[2048]{0:T(1024)} %param.21) | copy-start | bytes 24580
Sparse Core Ops, SparseCore 0:
  8.9 106.7 all-gather.1
where the time goes:
time: 299 us
  waiting for transfers between devices  97.2 us (33%)
  Pallas kernels  84.2 us (28%)
  matrix products  55 us (18%)
  blocking collectives  18.4 us (6%)
  between operations  14.8 us (5%)
  local copies, waits for them, and re-layouts  11.6 us (4%)
  other arithmetic  9.39 us (3%)
  starting transfers between devices  8.06 us (3%)
    all_gather x1, waiting for transfers between devices, shards(): piece = lax.all_gather(tokens, 'mp', axis=1, tiled=True)  94.3 us
    pallas_call x1, Pallas kernels, exchange(): pl.pallas_call(functools.partial(exchange_kernel, heads, zs), in_specs=[v...  48.7 us
    dot_general x1, matrix products, shards(): xp = jnp.dot(piece, w_x, preferred_element_type=F32).astype(BF16)  23.7 us
    dot_general x1, matrix products, shards(): gate = jnp.dot(piece, w_z, preferred_element_type=F32).astype(BF16)  23.7 us
    pallas_call x1, Pallas kernels, local_part(): pl.pallas_call(functools.partial(local_kernel, heads), grid=(blocks,), in...  20.2 us
    psum x1, blocking collectives, shards(): squares = lax.psum(sq, 'mp')  18.4 us
    pallas_call x1, Pallas kernels, finish(): pl.pallas_call(functools.partial(finish_kernel, heads), grid=(blocks,), i...  15.4 us
    dot_general x1, matrix products, shards(): small = jnp.dot(piece, w_small, preferred_element_type=F32)  7.59 us
  transfers between devices with their start and end apart: 5, of which 2 were waited for; matrix products, arithmetic and copies ran while one was open for 11% of the time, Pallas kernels for 0%

commit v1 on v0

--- a/solution.py
+++ b/solution.py
@@ -17,6 +17,227 @@
 BF16 = jnp.bfloat16
 
 
+TILE = 512
+
+
+def project_kernel(
+    mp, seqs, tok_ref, wx_ref, wz_ref, ws_ref,
+    xp_ref, gate_ref, bc_ref, raw_ref, halo_ref,
+    tok_v, wx_v, wz_v, ws_v, acc_x, acc_z, acc_s, stage_x, stage_z, edges, landed,
+    own_sem, w_sem, send_sem, recv_sem, out_sem, edge_s, edge_r,
+):
+    me = lax.axis_index("mp")
+    at = lax.axis_index("seq")
+    tok, width = tok_ref.shape
+    chunks = tok // BLOCK
+    order = [0, chunks - 1] + list(range(1, chunks - 1))
+
+    def rows(c):
+        return pl.ds(c * BLOCK, BLOCK)
+
+    loads = [
+        pltpu.make_async_copy(src, dst, w_sem.at[n])
+        for n, (src, dst) in enumerate(((wx_ref, wx_v), (ws_ref, ws_v), (wz_ref, wz_v)))
+    ]
+    owns = [
+        pltpu.make_async_copy(tok_ref.at[rows(c)], tok_v.at[me, rows(c)], own_sem.at[c])
+        for c in range(chunks)
+    ]
+    barrier = pltpu.get_barrier_semaphore()
+    for k in range(1, mp):
+        pl.semaphore_signal(
+            barrier, inc=1, device_id={"mp": lax.rem(me + k, mp)}, device_id_type=MESH
+        )
+
+    for other in (lax.rem(at + 1, seqs), lax.rem(at + seqs - 1, seqs)):
+        pl.semaphore_signal(barrier, inc=1, device_id={"seq": other}, device_id_type=MESH)
+    owns[order[0]].start()
+    loads[0].start()
+    pl.semaphore_wait(barrier, mp - 1 + 2)
+
+    def sends(c):
+        return [
+            pltpu.make_async_remote_copy(
+                src_ref=tok_ref.at[rows(c)], dst_ref=tok_v.at[me, rows(c)],
+                send_sem=send_sem.at[k, c], recv_sem=recv_sem.at[k, c],
+                device_id={"mp": lax.rem(me + k, mp)}, device_id_type=MESH,
+            )
+            for k in range(1, mp)
+        ]
+
+    def arrival(c, k):
+        source = lax.rem(me - k + mp, mp)
+        return source, pltpu.make_async_remote_copy(
+            src_ref=tok_ref.at[rows(c)], dst_ref=tok_v.at[source, rows(c)],
+            send_sem=send_sem.at[k, c], recv_sem=recv_sem.at[k, c],
+            device_id={"mp": source}, device_id_type=MESH,
+        )
+
+    def edge(way, to):
+        return pltpu.make_async_remote_copy(
+            src_ref=edges.at[way], dst_ref=landed.at[way],
+            send_sem=edge_s.at[way], recv_sem=edge_r.at[way],
+            device_id={"seq": to}, device_id_type=MESH,
+        )
+
+    going = sends(order[0])
+    for copy in going:
+        copy.start()
+    loads[1].start()
+    loads[2].start()
+    for c in order[1:]:
+        owns[c].start()
+
+    def out(c, slot, which):
+        stage, to = (stage_x, xp_ref) if which == 0 else (stage_z, gate_ref)
+        return pltpu.make_async_copy(stage.at[slot], to.at[rows(c)], out_sem.at[which, slot])
+
+    for n, c in enumerate(order):
+        slot = n % 2
+
+        def contract(source, weights, acc, stage, first, last):
+            depth = pl.ds(pl.multiple_of(source * width, width), width)
+            tile = min(TILE, weights.shape[1])
+
+            @pl.loop(0, weights.shape[1] // tile)
+            def _(t):
+                cols = pl.ds(pl.multiple_of(t * tile, tile), tile)
+                part = jnp.dot(
+                    tok_v[source, rows(c), :], weights[depth, cols], preferred_element_type=F32
+                )
+                if not first:
+                    part = part + acc[:, cols]
+                if last:
+                    stage[slot, :, cols] = part.astype(BF16)
+                else:
+                    acc[:, cols] = part
+
+        def contract_small(source, first):
+            depth = pl.ds(pl.multiple_of(source * width, width), width)
+            part = jnp.dot(tok_v[source, rows(c), :], ws_v[depth, :], preferred_element_type=F32)
+            acc_s[...] = part if first else acc_s[...] + part
+
+        owns[c].wait()
+        if n == 0:
+            loads[0].wait()
+        contract(me, wx_v, acc_x, stage_x, True, False)
+        if n == 0:
+            loads[1].wait()
+        contract_small(me, True)
+        if n == 0:
+            loads[2].wait()
+        contract(me, wz_v, acc_z, stage_z, True, False)
+        for copy in going:
+            copy.wait_send()
+        if n + 1 < chunks:
+            going = sends(order[n + 1])
+            for copy in going:
+                copy.start()
+        if n >= 2:
+            for which in range(2):
+                out(order[n - 2], slot, which).wait()
+        sources = []
+        for k in range(1, mp):
+            source, copy = arrival(c, k)
+            copy.wait_recv()
+            sources.append(source)
+            contract(source, wx_v, acc_x, stage_x, False, k == mp - 1)
+            contract_small(source, False)
+        out(c, slot, 0).start()
+        bc_ref[rows(c), :] = acc_s[:, :2 * LANES].astype(BF16)
+        raw_ref[rows(c), :] = acc_s[:, 2 * LANES:]
+        inner = stage_x.shape[2]
+        if n == 0:
+            edges[0, :, :inner] = stage_x[slot, :16, :]
+            edges[0, :, inner:] = acc_s[:16, :2 * LANES].astype(BF16)
+        if n == 1:
+            edges[1, :, :inner] = stage_x[slot, BLOCK - 16:, :]
+            edges[1, :, inner:] = acc_s[BLOCK - 16:, :2 * LANES].astype(BF16)
+
+            @pl.when(at > 0)
+            def _():
+                edge(0, at - 1).start()
+
+            @pl.when(at < seqs - 1)
+            def _():
+                edge(1, at + 1).start()
+
+        for k, source in enumerate(sources):
+            contract(source, wz_v, acc_z, stage_z, False, k == mp - 2)
+        out(c, slot, 1).start()
+
+    @pl.when(at > 0)
+    def _():
+        edge(1, at - 1).wait_recv()
+        halo_ref[0] = landed[1]
+        edge(0, at - 1).wait_send()
+
+    @pl.when(at == 0)
+    def _():
+        halo_ref[0] = jnp.zeros(halo_ref.shape[1:], BF16)
+
+    @pl.when(at < seqs - 1)
+    def _():
+        edge(0, at + 1).wait_recv()
+        halo_ref[1] = landed[0]
+        edge(1, at + 1).wait_send()
+
+    @pl.when(at == seqs - 1)
+    def _():
+        halo_ref[1] = jnp.zeros(halo_ref.shape[1:], BF16)
+
+    for n in range(max(0, chunks - 2), chunks):
+        for which in range(2):
+            out(order[n], n % 2, which).wait()
+
+
+def project(tokens, w_x, w_z, w_small):
+    tok, width = tokens.shape
+    inner = w_x.shape[1]
+    mp = lax.axis_size("mp")
+    seqs = lax.axis_size("seq")
+    chunks = tok // BLOCK
+    dma = pltpu.SemaphoreType.DMA
+    anywhere = pl.BlockSpec(memory_space=pl.ANY)
+    vmem = pl.BlockSpec(memory_space=pltpu.VMEM)
+    small = w_small.shape[1]
+    return pl.pallas_call(
+        functools.partial(project_kernel, mp, seqs),
+        in_specs=[anywhere] * 4,
+        out_specs=[anywhere, anywhere, vmem, vmem, vmem],
+        out_shape=[
+            jax.ShapeDtypeStruct((tok, inner), BF16),
+            jax.ShapeDtypeStruct((tok, inner), BF16),
+            jax.ShapeDtypeStruct((tok, 2 * LANES), BF16),
+            jax.ShapeDtypeStruct((tok, small - 2 * LANES), F32),
+            jax.ShapeDtypeStruct((2, 16, inner + 2 * LANES), BF16),
+        ],
+        scratch_shapes=[
+            pltpu.VMEM((mp, tok, width), BF16),
+            pltpu.VMEM(w_x.shape, BF16),
+            pltpu.VMEM(w_z.shape, BF16),
+            pltpu.VMEM(w_small.shape, BF16),
+            pltpu.VMEM((BLOCK, inner), F32),
+            pltpu.VMEM((BLOCK, inner), F32),
+            pltpu.VMEM((BLOCK, small), F32),
+            pltpu.VMEM((2, BLOCK, inner), BF16),
+            pltpu.VMEM((2, BLOCK, inner), BF16),
+            pltpu.VMEM((2, 16, inner + 2 * LANES), BF16),
+            pltpu.VMEM((2, 16, inner + 2 * LANES), BF16),
+            dma((chunks,)), dma((3,)), dma((mp, chunks)), dma((mp, chunks)), dma((2, 2)),
+            dma((2,)), dma((2,)),
+        ],
+        compiler_params=pltpu.CompilerParams(
+            collective_id=2, has_side_effects=True, vmem_limit_bytes=VMEM_LIMIT
+        ),
+        cost_estimate=pl.CostEstimate(
+            flops=2 * tok * width * mp * (2 * inner + small),
+            bytes_accessed=width * mp * (2 * inner + small) * 2, transcendentals=0,
+        ),
+        name="gather_and_project",
+    )(tokens, w_x, w_z, w_small)
+
+
 def silu(v):
     return v / (1.0 + jnp.exp(-v))
 
@@ -30,7 +251,7 @@
 
 
 def local_kernel(
-    heads, x_ref, bc_ref, prev_ref, next_ref, raw_ref, bias_ref, rate_ref, aux_ref, seg_ref,
+    heads, x_ref, bc_ref, xl_ref, xr_ref, bl_ref, br_ref, halo_ref, raw_ref, bias_ref, rate_ref, aux_ref, seg_ref,
     taps_ref, taps_bc_ref,
     inside_ref, c_ref, opf_ref, opb_ref, sf_ref, sb_ref, dec_ref, tot_ref, totdec_ref,
     accf, accb, run,
@@ -43,6 +264,15 @@
         accf[...] = jnp.zeros_like(accf)
         accb[...] = jnp.zeros_like(accb)
         run[...] = jnp.ones_like(run)
+
+    at_left = step == 0
+    at_right = step == pl.num_programs(0) - 1
+
+    def beside(left, right, cols):
+        left_halo, right_halo = halo_ref[0, :, cols], halo_ref[1, :, cols]
+        prev = jnp.where(at_left, left_halo.astype(F32), left.astype(F32))[15:16]
+        nxt = jnp.where(at_right, right_halo.astype(F32), right.astype(F32))[0:1]
+        return prev, nxt
 
     aux = aux_ref[...]
     seg_col, m_prev, m_next = aux[:, 0:1], aux[:, 1:2], aux[:, 2:3]
@@ -68,10 +298,8 @@
     dec_ref[0] = jnp.concatenate([dec_f, dec_b, jnp.zeros((6, LANES), F32)], axis=0)
     incl_t, excl_t, dt_t = incl.T, excl.T, dt.T
 
-    bcs = filtered(
-        bc_ref[...].astype(F32), prev_ref[0][:, inner:], next_ref[0][:, inner:], m_prev, m_next,
-        taps_bc_ref[...],
-    )
+    prev, nxt = beside(bl_ref[...], br_ref[...], slice(inner, inner + 2 * LANES))
+    bcs = filtered(bc_ref[...].astype(F32), prev, nxt, m_prev, m_next, taps_bc_ref[...])
     c_vecs = bcs[:, LANES:]
     c_ref[...] = c_vecs
     b_t = bcs[:, :LANES].astype(F32).T.astype(BF16)
@@ -81,10 +309,8 @@
     run_b = run[...]
     for h in range(heads):
         cols = slice(h * LANES, (h + 1) * LANES)
-        xs = filtered(
-            x_ref[:, cols].astype(F32), prev_ref[0][:, cols], next_ref[0][:, cols], m_prev, m_next,
-            taps_ref[:, cols],
-        )
+        prev, nxt = beside(xl_ref[:, cols], xr_ref[:, cols], cols)
+        xs = filtered(x_ref[:, cols].astype(F32), prev, nxt, m_prev, m_next, taps_ref[:, cols])
         one = slice(h, h + 1)
         gap = jnp.where(lower, incl[:, one] - incl_t[one], excl_t[one] - excl[:, one])
         weights = (scores * jnp.exp2(gap) * dt_t[one]).astype(BF16)
@@ -107,13 +333,16 @@
         totdec_ref[...] = run_b * dec_ref[0]
 
 
-def local_part(xp, bc, prev, nxt, raw, bias, rate, aux, seg_rows, taps, taps_bc, heads):
+def local_part(xp, bc, halo, raw, bias, rate, aux, seg_rows, taps, taps_bc, heads):
     tok, inner = xp.shape
     blocks = tok // BLOCK
     part = LANES // GROUP
     row = lambda b: (b, 0)
     lead = lambda b: (b, 0, 0)
     fixed = lambda b: (0, 0)
+    per = BLOCK // 16
+    left = lambda b: (jnp.maximum(b * per - 1, 0), 0)
+    right = lambda b: (jnp.minimum((b + 1) * per, tok // 16 - 1), 0)
     flops = tok * heads * (2 * BLOCK * LANES + 4 * LANES * LANES)
     return pl.pallas_call(
         functools.partial(local_kernel, heads),
@@ -121,8 +350,11 @@
         in_specs=[
             pl.BlockSpec((BLOCK, inner), row),
             pl.BlockSpec((BLOCK, 2 * LANES), row),
-            pl.BlockSpec((1, 1, inner + 2 * LANES), lead),
-            pl.BlockSpec((1, 1, inner + 2 * LANES), lead),
+            pl.BlockSpec((16, inner), left),
+            pl.BlockSpec((16, inner), right),
+            pl.BlockSpec((16, 2 * LANES), left),
+            pl.BlockSpec((16, 2 * LANES), right),
+            pl.BlockSpec((2, 16, inner + 2 * LANES), lambda b: (0, 0, 0)),
             pl.BlockSpec((BLOCK, LANES), row),
             pl.BlockSpec((1, LANES), fixed),
             pl.BlockSpec((1, LANES), fixed),
@@ -166,7 +398,7 @@
             transcendentals=tok * BLOCK * heads,
         ),
         name="local_part",
-    )(xp, bc, prev, nxt, raw, bias, rate, aux, seg_rows, taps, taps_bc)
+    )(xp, bc, xp, xp, bc, bc, halo, raw, bias, rate, aux, seg_rows, taps, taps_bc)
 
 
 def spread(row, heads):
@@ -494,22 +726,9 @@
     bias = jnp.pad(dt_bias, (0, LANES - heads))[None]
     rate = jnp.pad(rates, (0, LANES - heads))[None]
 
-    piece = lax.all_gather(tokens, "mp", axis=1, tiled=True)
-    small = jnp.dot(piece, w_small, preferred_element_type=F32)
-    bc = small[:, :2 * LANES].astype(BF16)
-    raw = small[:, 2 * LANES:]
-    xp = jnp.dot(piece, w_x, preferred_element_type=F32).astype(BF16)
-    gate = jnp.dot(piece, w_z, preferred_element_type=F32).astype(BF16)
-
-    firsts = jnp.concatenate([xp[::BLOCK], bc[::BLOCK]], axis=1).astype(F32)
-    lasts = jnp.concatenate([xp[BLOCK - 1::BLOCK], bc[BLOCK - 1::BLOCK]], axis=1).astype(F32)
-    from_left = lax.ppermute(lasts[-1:], "seq", [(i, i + 1) for i in range(seq_count - 1)])
-    from_right = lax.ppermute(firsts[:1], "seq", [(i + 1, i) for i in range(seq_count - 1)])
-    prev = jnp.concatenate([from_left, lasts[:-1]], axis=0)[:, None]
-    nxt = jnp.concatenate([firsts[1:], from_right], axis=0)[:, None]
-
+    xp, gate, bc, raw, halo = project(tokens, w_x, w_z, w_small)
     inside, c_vecs, opf, opb, sf, sb, dec, tot, totdec = local_part(
-        xp, bc, prev, nxt, raw, bias, rate, aux, seg_rows, conv_x, conv_bc, heads
+        xp, bc, halo, raw, bias, rate, aux, seg_rows, conv_x, conv_bc, heads
     )
     ent = exchange(tot, totdec, heads)
     gated, sq = finish(inside, c_vecs, opf, opb, gate, sf, sb, dec, ent, heads)

time: 299 us -> 230 us (0.77)
  Pallas kernels: 84.2 us -> 187 us
  waiting for transfers between devices: 97.2 us -> 0.01 us
  matrix products: 55 us -> 0 us
  between operations: 14.8 us -> 1.27 us
  local copies, waits for them, and re-layouts: 11.6 us -> 5.11 us
  starting transfers between devices: 8.06 us -> 4.79 us
    pallas_call x0 -> x1, Pallas kernels: none -> 104 us  [project(): pl.pallas_call(functools.partial(project_kernel, mp, seqs), in_specs=[any...]
    all_gather x1 -> x0, waiting for transfers between devices: 94.3 us -> none  [shards(): piece = lax.all_gather(tokens, 'mp', axis=1, tiled=True)]
    dot_general x3 -> x0, matrix products: 55 us -> none  [the longest x1 23.7 us: shards(): xp = jnp.dot(piece, w_x, preferred_element_type=F32).astype(BF16)]
    slice x7 -> x0, local copies, waits for them, and re-layouts: 5.17 us -> none  [the longest x2 2.28 us: shards(): firsts = jnp.concatenate([xp[::BLOCK], bc[::BLOCK]], axis=1).astype(F32)]
    concatenate x1, other arithmetic: 0.02 us -> 3.72 us  [shards(): jnp.concatenate([w_bc, jnp.pad(w_dt, ((0, 0), (0, LANES - heads)))], axis=1)]
    ppermute x2 -> x0, starting transfers between devices: 3.23 us -> none  [the longest x1 1.77 us: shards(): lax.ppermute(lasts[-1:], 'seq', [(i, i + 1) for i in range(seq_count - 1)])]
  transfers between devices with their start and end apart: 5 -> 2, of which waited for: 2 -> 0; matrix products, arithmetic and copies ran while one was open for 11% -> 3% of each run, Pallas kernels for 0% -> 45%
where the time goes in v1:
time: 230 us; the launch traced here: 229 us
  Pallas kernels  187 us (81%)
  blocking collectives  20.3 us (9%)
  other arithmetic  10.9 us (5%)
  local copies, waits for them, and re-layouts  5.11 us (2%)
  starting transfers between devices  4.79 us (2%)
    pallas_call x1, Pallas kernels, project(): pl.pallas_call(functools.partial(project_kernel, mp, seqs), in_specs=[any...  104 us
    pallas_call x1, Pallas kernels, exchange(): pl.pallas_call(functools.partial(exchange_kernel, heads, zs), in_specs=[v...  47.1 us
    pallas_call x1, Pallas kernels, local_part(): pl.pallas_call(functools.partial(local_kernel, heads), grid=(blocks,), in...  20.6 us
    psum x1, blocking collectives, shards(): squares = lax.psum(sq, 'mp')  20.3 us
    pallas_call x1, Pallas kernels, finish(): pl.pallas_call(functools.partial(finish_kernel, heads), grid=(blocks,), i...  15.5 us
    convert_element_type x1, other arithmetic, shards(): return (gated * scale * norm_gain).astype(BF16)  6.15 us
  transfers between devices with their start and end apart: 2, of which 0 were waited for; matrix products, arithmetic and copies ran while one was open for 3% of the time, Pallas kernels for 45%

profile of v1, /device:TPU:0, one launch (start us, length us, event | category | flops | bytes accessed | tf_op | source)
XLA Modules:
  0.0 229.4 jit_solution(8870387543612515238)
XLA Ops:
  0.0 0.7 convert_element_type.7
  0.7 0.0 copy-start
  0.7 0.6 fusion.3
  1.3 1.3 collective-permute-start.1
  2.6 3.5 %collective-permute-start = (f32[1]{0:T(128)}, f32[1]{0:T(128)}, u32[]{:S(2)}, u32[]{:S(2)}) collective-permute-start(f32[1]{0:T(128)} %get-tuple-element.47), channel_id=1, source_target_pairs={{0,2},{2,4},{4,6},{6,8},{8,10},{10,12},{12,14},{14,16},{16,18},{18... | collective-permute-start | bytes 20 | tf_op jit(solution)/shard_map/ppermute | solution.py:690
  6.1 0.1 slice.31
  6.2 0.1 slice.30
  6.3 0.1 fusion.2
  6.3 0.1 broadcast_bitcast_fusion.1
  6.4 0.1 broadcast_bitcast_fusion
  6.5 1.4 copy.22
  7.9 1.3 pad_bitcast_fusion
  9.2 3.7 %fusion.1.ws_ref = bf16[4096,384]{1,0:T(8,128)(2,1)} fusion(bf16[4096,16]{1,0:T(8,128)(2,1)S(1)} %copy.22, bf16[4096,256]{1,0:T(8,128)(2,1)} %param.15), kind=kLoop, calls=%fused_computation.3 | loop fusion | flops 9437184 | bytes 5373952 | tf_op jit(solution)/shard_map/concatenate | solution.py:725
  12.9 0.0 copy-start.1
  12.9 103.8 %gather_and_project.1 = (bf16[1024,2048]{1,0:T(8,128)(2,1)}, bf16[1024,2048]{1,0:T(8,128)(2,1)}, bf16[1024,256]{1,0:T(8,128)(2,1)}, f32[1024,128]{1,0:T(8,128)}, bf16[2,16,2304]{2,1,0:T(8,128)(2,1)}) custom-call(bf16[1024,2048]{1,0:T(8,128)(2,1)} %tok_ref.1, bf16[4096,2048]{1,0:T(8,128)(2,1)} %wx_ref.1, bf16[4096,2048]{1,0:T(8,128)(2,1)} %wz_ref.1, ...), custom_call_target="tpu_custom_call" | custom-call | flops 37580963840 | bytes 36700160 | tf_op jit(solution)/shard_map/gather_and_project/pallas_call | solution.py:204
  116.7 0.0 collective-permute-done.1
  117.3 0.0 copy-done.1
  117.3 0.1 compare_convert_fusion.4
  117.4 0.1 slice.29
  117.5 0.1 broadcast_bitcast_fusion.2
  117.6 0.0 collective-permute-done
  118.1 0.1 compare_convert_fusion.5
  118.2 0.1 slice.28
  118.3 0.1 broadcast_bitcast_fusion.3
  118.4 0.0 copy-done
  118.4 0.1 stack.56
  118.4 1.0 copy.23.aux_ref
  119.5 20.6 %local_part.1 = (f32[1024,2048]{1,0:T(8,128)}, bf16[1024,128]{1,0:T(8,128)(2,1)}, f32[1024,128]{1,0:T(8,128)}, f32[1024,128]{1,0:T(8,128)}, f32[4,128,2048]{2,1,...) custom-call(bf16[1024,2048]{1,0:T(8,128)(2,1)} %get-tuple-element.21, ...), custom_call_target="tpu_custom_call" | custom-call | flops 2147483648 | bytes 20971520 | tf_op jit(solution)/shard_map/local_part/pallas_call | solution.py:347
  140.1 47.1 %exchange_states.1.ent_ref = bf16[4,2,32,2048]{3,2,1,0:T(8,128)(2,1)} custom-call(bf16[4,2,32,2048]{3,2,1,0:T(8,128)(2,1)} %get-tuple-element.33.tot_ref, f32[8,128]{1,0:T(8,128)} %get-tuple-element.34.dec_ref), custom_call_target="tpu_custom_call" | custom-call | flops 10485760 | bytes 4194304 | tf_op jit(solution)/shard_map/exchange_states/pallas_call | solution.py:580
  187.2 0.0 copy-start.2
  187.2 15.5 %finish.1 = (f32[1024,2048]{1,0:T(8,128)}, f32[1024,1]{1,0:T(8,128)}) custom-call(f32[1024,2048]{1,0:T(8,128)} %get-tuple-element.25.inside_ref, bf16[1024,128]{1,0:T(8,128)(2,1)} %get-tuple-element.26.c_ref, f32[1024,128]{1,0:T(8,128)} %get-tuple-element.27.opf_ref, f32[1024,128]{1,0:T(8,128)} %get-tuple-element.28.opb_ref, ...), custom_call_target="tpu_custom_call" | custom-call | flops 1073741824 | bytes 20971520 | tf_op jit(solution)/shard_map/finish/pallas_call | solution.py:654
  202.7 20.3 %psum.7 = f32[1024,1]{1,0:T(8,128)S(1)} all-reduce(f32[1024,1]{1,0:T(8,128)} %get-tuple-element.36), channel_id=1, replica_groups=mesh['seq'=16,'mp'=2] {'mp'}, use_global_device_ids=true, to_apply=%region_0.1 | all-reduce | flops 1024 | bytes 8192 | tf_op jit(solution)/shard_map/psum | solution.py:735
  223.0 0.2 rsqrt_reduce_fusion
  223.3 0.0 copy-done.2
  223.3 6.1 %multiply_convert_fusion = bf16[1024,2048]{1,0:T(8,128)(2,1)} fusion(f32[1024,2048]{1,0:T(8,128)} %get-tuple-element.35, f32[2048]{0:T(1024)S(1)} %copy-done.2, f32[1024]{0:T(1024)S(1)} %rsqrt_reduce_fusion), kind=kLoop, calls=%fused_computation | loop fusion | flops 6291456 | bytes 12595200 | tf_op jit(solution)/shard_map/convert_element_type | solution.py:737
  (5 shorter events, 0.0 us)
Async XLA Ops:
  0.7 117.7 %copy-start = (f32[1024]{0:T(1024)}, f32[1024]{0:T(1024)S(1)}, u32[]{:S(2)}) copy-start(f32[1024]{0:T(1024)S(1)} %convert_element_type.7) | copy-start | bytes 12292
  1.3 115.4 %collective-permute-start.1 = (f32[1]{0:T(128)}, f32[1]{0:T(128)}, u32[]{:S(2)}, u32[]{:S(2)}) collective-permute-start(f32[1]{0:T(128)} %get-tuple-element.46), channel_id=1, source_target_pairs={{2,0},{4,2},{6,4},{8,6},{10,8},{12,10},{14,12},{16,14},{18,16},{20... | collective-permute-start | bytes 20 | tf_op jit(solution)/shard_map/ppermute | solution.py:691
  2.6 115.0 %collective-permute-start = (f32[1]{0:T(128)}, f32[1]{0:T(128)}, u32[]{:S(2)}, u32[]{:S(2)}) collective-permute-start(f32[1]{0:T(128)} %get-tuple-element.47), channel_id=1, source_target_pairs={{0,2},{2,4},{4,6},{6,8},{8,10},{10,12},{12,14},{14,16},{16,18},{18... | collective-permute-start | bytes 20 | tf_op jit(solution)/shard_map/ppermute | solution.py:690
  12.9 104.4 %copy-start.1 = (s32[1024]{0:T(1024)S(1)}, s32[1024]{0:T(1024)}, u32[]{:S(2)}) copy-start(s32[1024]{0:T(1024)} %param.12) | copy-start | bytes 12292
  187.2 36.0 %copy-start.2 = (f32[2048]{0:T(1024)S(1)}, f32[2048]{0:T(1024)}, u32[]{:S(2)}) copy-start(f32[2048]{0:T(1024)} %param.21) | copy-start | bytes 24580

commit v2 on v1

--- a/solution.py
+++ b/solution.py
@@ -21,7 +21,7 @@
 
 
 def project_kernel(
-    mp, seqs, tok_ref, wx_ref, wz_ref, ws_ref,
+    mp, seqs, tok_ref, wx_ref, wz_ref, wbc_ref, wdt_ref,
     xp_ref, gate_ref, bc_ref, raw_ref, halo_ref,
     tok_v, wx_v, wz_v, ws_v, acc_x, acc_z, acc_s, stage_x, stage_z, edges, landed,
     own_sem, w_sem, send_sem, recv_sem, out_sem, edge_s, edge_r,
@@ -37,7 +37,14 @@
 
     loads = [
         pltpu.make_async_copy(src, dst, w_sem.at[n])
-        for n, (src, dst) in enumerate(((wx_ref, wx_v), (ws_ref, ws_v), (wz_ref, wz_v)))
+        for n, (src, dst) in enumerate(
+            (
+                (wx_ref, wx_v),
+                (wbc_ref, ws_v.at[:, :2 * LANES]),
+                (wdt_ref, ws_v.at[:, 2 * LANES:]),
+                (wz_ref, wz_v),
+            )
+        )
     ]
     owns = [
         pltpu.make_async_copy(tok_ref.at[rows(c)], tok_v.at[me, rows(c)], own_sem.at[c])
@@ -83,8 +90,8 @@
     going = sends(order[0])
     for copy in going:
         copy.start()
-    loads[1].start()
-    loads[2].start()
+    for load in loads[1:]:
+        load.start()
     for c in order[1:]:
         owns[c].start()
 
@@ -123,9 +130,10 @@
         contract(me, wx_v, acc_x, stage_x, True, False)
         if n == 0:
             loads[1].wait()
+            loads[2].wait()
         contract_small(me, True)
         if n == 0:
-            loads[2].wait()
+            loads[3].wait()
         contract(me, wz_v, acc_z, stage_z, True, False)
         for copy in going:
             copy.wait_send()
@@ -191,7 +199,7 @@
             out(order[n], n % 2, which).wait()
 
 
-def project(tokens, w_x, w_z, w_small):
+def project(tokens, w_x, w_z, w_bc, w_steps):
     tok, width = tokens.shape
     inner = w_x.shape[1]
     mp = lax.axis_size("mp")
@@ -200,10 +208,10 @@
     dma = pltpu.SemaphoreType.DMA
     anywhere = pl.BlockSpec(memory_space=pl.ANY)
     vmem = pl.BlockSpec(memory_space=pltpu.VMEM)
-    small = w_small.shape[1]
+    small = w_bc.shape[1] + w_steps.shape[1]
     return pl.pallas_call(
         functools.partial(project_kernel, mp, seqs),
-        in_specs=[anywhere] * 4,
+        in_specs=[anywhere] * 5,
         out_specs=[anywhere, anywhere, vmem, vmem, vmem],
         out_shape=[
             jax.ShapeDtypeStruct((tok, inner), BF16),
@@ -216,7 +224,7 @@
             pltpu.VMEM((mp, tok, width), BF16),
             pltpu.VMEM(w_x.shape, BF16),
             pltpu.VMEM(w_z.shape, BF16),
-            pltpu.VMEM(w_small.shape, BF16),
+            pltpu.VMEM((w_x.shape[0], small), BF16),
             pltpu.VMEM((BLOCK, inner), F32),
             pltpu.VMEM((BLOCK, inner), F32),
             pltpu.VMEM((BLOCK, small), F32),
@@ -224,7 +232,7 @@
             pltpu.VMEM((2, BLOCK, inner), BF16),
             pltpu.VMEM((2, 16, inner + 2 * LANES), BF16),
             pltpu.VMEM((2, 16, inner + 2 * LANES), BF16),
-            dma((chunks,)), dma((3,)), dma((mp, chunks)), dma((mp, chunks)), dma((2, 2)),
+            dma((chunks,)), dma((4,)), dma((mp, chunks)), dma((mp, chunks)), dma((2, 2)),
             dma((2,)), dma((2,)),
         ],
         compiler_params=pltpu.CompilerParams(
@@ -235,7 +243,7 @@
             bytes_accessed=width * mp * (2 * inner + small) * 2, transcendentals=0,
         ),
         name="gather_and_project",
-    )(tokens, w_x, w_z, w_small)
+    )(tokens, w_x, w_z, w_bc, w_steps)
 
 
 def silu(v):
@@ -449,15 +457,22 @@
             device_id={"seq": to}, device_id_type=MESH,
         )
 
-    firsts = []
+    def near_copy(r, way):
+        return send(
+            tot_ref.at[members[r], way], near.at[r, way], near_s.at[r, way], near_r.at[r, way],
+            z * GROUP + members[r],
+        )
+
+    def dec_copy(r):
+        return send(dec_ref, near_dec.at[r], dec_s.at[r], dec_r.at[r], z * GROUP + members[r])
+
     for r in range(1, GROUP):
-        to = z * GROUP + members[r]
-        firsts.append(send(dec_ref, near_dec.at[r], dec_s.at[r], dec_r.at[r], to))
-        firsts.append(send(tot_ref.at[members[r]], near.at[r], near_s.at[r], near_r.at[r], to))
-    for copy in firsts:
-        copy.start()
-    for copy in firsts:
-        copy.wait()
+        dec_copy(r).start()
+    for way in range(2):
+        for r in range(1, GROUP):
+            near_copy(r, way).start()
+    for r in range(1, GROUP):
+        dec_copy(r).wait()
 
     decs = [dec_ref[...]] + [near_dec[r] for r in range(1, GROUP)]
 
@@ -485,43 +500,52 @@
             terms.append(jnp.where(inside, decs[k][way:way + 1], 1.0))
         return product(terms)
 
+    sums_dec[...] = product(decs)
+
+    def far_copies(way, d):
+        to = (z + d if way == 0 else z - d) * GROUP + i
+        ssem, rsem = (f_s, f_r) if way == 0 else (b_s, b_r)
+        far = far_b if way else far_f
+        return (
+            send(sums_dec, far_dec.at[way, d], fd_s.at[way, d], fd_r.at[way, d], to),
+            send(sums.at[way], far.at[d], ssem.at[d], rsem.at[d], to),
+        )
+
+    def sends_far(way, d):
+        return z + d < zs if way == 0 else z - d >= 0
+
+    def gets_far(way, d):
+        return z - d >= 0 if way == 0 else z + d < zs
+
     for way in range(2):
+        for r in range(1, GROUP):
+            near_copy(r, way).wait()
         total = jnp.zeros(sums.shape[1:], F32)
         for r in range(GROUP):
             total = total + spread(beyond(r, way), heads) * state(r, way)
         sums[way] = total.astype(BF16)
-    sums_dec[...] = product(decs)
-
-    for d in range(1, zs):
-        up = (z + d) * GROUP + i
-        down = (z - d) * GROUP + i
-
-        @pl.when(z + d < zs)
-        def _():
-            send(sums_dec, far_dec.at[0, d], fd_s.at[0, d], fd_r.at[0, d], up).start()
-            send(sums.at[0], far_f.at[d], f_s.at[d], f_r.at[d], up).start()
-
-        @pl.when(z - d >= 0)
-        def _():
-            send(sums_dec, far_dec.at[1, d], fd_s.at[1, d], fd_r.at[1, d], down).start()
-            send(sums.at[1], far_b.at[d], b_s.at[d], b_r.at[d], down).start()
-
-    for d in range(1, zs):
-        up = (z + d) * GROUP + i
-        down = (z - d) * GROUP + i
-
-        @pl.when(z - d >= 0)
-        def _():
-            send(sums_dec, far_dec.at[0, d], fd_s.at[0, d], fd_r.at[0, d], down).wait_recv()
-            send(sums.at[0], far_f.at[d], f_s.at[d], f_r.at[d], down).wait_recv()
-
-        @pl.when(z + d < zs)
-        def _():
-            send(sums_dec, far_dec.at[1, d], fd_s.at[1, d], fd_r.at[1, d], up).wait_recv()
-            send(sums.at[1], far_b.at[d], b_s.at[d], b_r.at[d], up).wait_recv()
+        for d in range(1, zs):
+
+            @pl.when(sends_far(way, d))
+            def _():
+                for copy in far_copies(way, d):
+                    copy.start()
+
+    def back_copy(r, way):
+        return send(
+            back.at[r, way], landed.at[r, way], back_s.at[r, way], back_r.at[r, way],
+            z * GROUP + members[r],
+        )
 
     for way in range(2):
         far = far_b if way else far_f
+        for d in range(1, zs):
+
+            @pl.when(gets_far(way, d))
+            def _():
+                for copy in far_copies(way, d):
+                    copy.wait_recv()
+
         entering = jnp.zeros(sums.shape[1:], F32)
         weight = jnp.ones((1, LANES), F32)
         for d in range(1, zs):
@@ -546,30 +570,21 @@
                     value = value + spread(weight, heads) * state(r, way)
             back[s, way] = value.astype(BF16)
 
-    lasts = []
-    for r in range(1, GROUP):
-        to = z * GROUP + members[r]
-        lasts.append(send(back.at[r], landed.at[r], back_s.at[r], back_r.at[r], to))
-    for copy in lasts:
-        copy.start()
+        for r in range(1, GROUP):
+            back_copy(r, way).start()
+
     ent_ref[i] = back[0]
     for r in range(1, GROUP):
-        lasts[r - 1].wait()
+        for way in range(2):
+            back_copy(r, way).wait()
         ent_ref[members[r]] = landed[r]
-
-    for d in range(1, zs):
-        up = (z + d) * GROUP + i
-        down = (z - d) * GROUP + i
-
-        @pl.when(z + d < zs)
-        def _():
-            send(sums_dec, far_dec.at[0, d], fd_s.at[0, d], fd_r.at[0, d], up).wait_send()
-            send(sums.at[0], far_f.at[d], f_s.at[d], f_r.at[d], up).wait_send()
-
-        @pl.when(z - d >= 0)
-        def _():
-            send(sums_dec, far_dec.at[1, d], fd_s.at[1, d], fd_r.at[1, d], down).wait_send()
-            send(sums.at[1], far_b.at[d], b_s.at[d], b_r.at[d], down).wait_send()
+    for way in range(2):
+        for d in range(1, zs):
+
+            @pl.when(sends_far(way, d))
+            def _():
+                for copy in far_copies(way, d):
+                    copy.wait_send()
 
 
 def exchange(tot, totdec, heads):
@@ -592,10 +607,10 @@
             pltpu.VMEM((2, zs, 8, LANES), F32),
             pltpu.VMEM((GROUP, 2, part, inner), BF16),
             pltpu.VMEM((GROUP, 2, part, inner), BF16),
-            dma((GROUP,)), dma((GROUP,)), dma((GROUP,)), dma((GROUP,)),
+            dma((GROUP, 2)), dma((GROUP, 2)), dma((GROUP,)), dma((GROUP,)),
             dma((zs,)), dma((zs,)), dma((zs,)), dma((zs,)),
             dma((2, zs)), dma((2, zs)),
-            dma((GROUP,)), dma((GROUP,)),
+            dma((GROUP, 2)), dma((GROUP, 2)),
         ],
         compiler_params=pltpu.CompilerParams(
             collective_id=1, has_side_effects=True, vmem_limit_bytes=VMEM_LIMIT
@@ -608,11 +623,28 @@
 
 
 def finish_kernel(
-    heads, inside_ref, c_ref, opf_ref, opb_ref, gate_ref, sf_ref, sb_ref, dec_ref, decs_ref,
-    ent_ref, out_ref, sq_ref, hf, hb,
+    heads, mp, inside_ref, c_ref, opf_ref, opb_ref, gate_ref, sf_ref, sb_ref, dec_ref, decs_ref,
+    ent_ref, gain_ref, out_ref, hf, hb, held, sums, sent, got,
 ):
     step = pl.program_id(0)
     blocks = hb.shape[0]
+    me = lax.axis_index("mp")
+
+    def send(k, b):
+        return pltpu.make_async_remote_copy(
+            src_ref=sums.at[0, b], dst_ref=sums.at[k, b],
+            send_sem=sent.at[k, b], recv_sem=got.at[k, b],
+            device_id={"mp": lax.rem(me + k, mp)}, device_id_type=MESH,
+        )
+
+    @pl.when(step == 0)
+    def _():
+        barrier = pltpu.get_barrier_semaphore()
+        for k in range(1, mp):
+            pl.semaphore_signal(
+                barrier, inc=1, device_id={"mp": lax.rem(me + k, mp)}, device_id_type=MESH
+            )
+        pl.semaphore_wait(barrier, mp - 1)
     part = LANES // GROUP
 
     @pl.when(step == 0)
@@ -640,19 +672,39 @@
         mixed = inside_ref[:, cols] + got_f * opf[:, one] + got_b * opb[:, one]
         gated = mixed * silu(gate_ref[:, cols].astype(F32))
         squares = squares + gated * gated
-        out_ref[:, cols] = gated
-    sq_ref[...] = jnp.sum(squares, axis=1, keepdims=True)
-
-
-def finish(inside, c_vecs, opf, opb, gate, sf, sb, dec, ent, heads):
+        held[step, :, cols] = gated
+    sums[0, step] = jnp.broadcast_to(jnp.sum(squares.T, axis=0, keepdims=True), (8, BLOCK))
+    for k in range(1, mp):
+        send(k, step).start()
+
+    @pl.when(step == blocks - 1)
+    def _():
+        for b in range(blocks):
+            total = sums[0, b]
+            for k in range(1, mp):
+                send(k, b).wait_recv()
+                total = total + sums[k, b]
+            scale = lax.rsqrt(total[0:1] / (heads * LANES * mp) + 1e-05)
+            scale = jnp.broadcast_to(scale, (LANES, BLOCK)).T
+            for h in range(heads):
+                cols = slice(h * LANES, (h + 1) * LANES)
+                value = held[b, :, cols] * scale * gain_ref[:, cols]
+                out_ref[b * BLOCK:(b + 1) * BLOCK, cols] = value.astype(BF16)
+        for b in range(blocks):
+            for k in range(1, mp):
+                send(k, b).wait_send()
+
+
+def finish(inside, c_vecs, opf, opb, gate, sf, sb, dec, ent, gain, heads):
     tok, inner = inside.shape
     blocks = tok // BLOCK
     part = LANES // GROUP
     row = lambda b: (b, 0)
     lead = lambda b: (b, 0, 0)
     whole = lambda b: (0, 0, 0)
+    mp = lax.axis_size("mp")
     return pl.pallas_call(
-        functools.partial(finish_kernel, heads),
+        functools.partial(finish_kernel, heads, mp),
         grid=(blocks,),
         in_specs=[
             pl.BlockSpec((BLOCK, inner), row),
@@ -665,24 +717,27 @@
             pl.BlockSpec((1, 8, LANES), lead),
             pl.BlockSpec((blocks, 8, LANES), whole),
             pl.BlockSpec((GROUP, 2, part, inner), lambda b: (0, 0, 0, 0)),
-        ],
-        out_specs=[pl.BlockSpec((BLOCK, inner), row), pl.BlockSpec((BLOCK, 1), row)],
-        out_shape=[
-            jax.ShapeDtypeStruct((tok, inner), F32),
-            jax.ShapeDtypeStruct((tok, 1), F32),
-        ],
+            pl.BlockSpec((1, inner), lambda b: (0, 0)),
+        ],
+        out_specs=pl.BlockSpec((tok, inner), lambda b: (0, 0)),
+        out_shape=jax.ShapeDtypeStruct((tok, inner), BF16),
         scratch_shapes=[
             pltpu.VMEM((LANES, inner), F32),
             pltpu.VMEM((blocks, LANES, inner), BF16),
+            pltpu.VMEM((blocks, BLOCK, inner), F32),
+            pltpu.VMEM((mp, blocks, 8, BLOCK), F32),
+            pltpu.SemaphoreType.DMA((mp, blocks)),
+            pltpu.SemaphoreType.DMA((mp, blocks)),
         ],
         compiler_params=pltpu.CompilerParams(
-            dimension_semantics=("arbitrary",), vmem_limit_bytes=VMEM_LIMIT
+            dimension_semantics=("arbitrary",), vmem_limit_bytes=VMEM_LIMIT,
+            collective_id=3, has_side_effects=True,
         ),
         cost_estimate=pl.CostEstimate(
             flops=tok * inner * LANES * 4, bytes_accessed=tok * inner * 10, transcendentals=tok * inner
         ),
         name="finish",
-    )(inside, c_vecs, opf, opb, gate, sf, sb, dec, dec, ent)
+    )(inside, c_vecs, opf, opb, gate, sf, sb, dec, dec, ent, gain[None])
 
 
 def neighbours(rows):
@@ -696,7 +751,6 @@
     tok = tokens.shape[0]
     inner = w_x.shape[1]
     heads = w_dt.shape[1]
-    mp_count = lax.axis_size("mp")
     seq_count = lax.axis_size("seq")
     position = lax.axis_index("seq")
     blocks = tok // BLOCK
@@ -722,19 +776,16 @@
         axis=1,
     )
     seg_rows = seg.reshape(blocks, 1, BLOCK)
-    w_small = jnp.concatenate([w_bc, jnp.pad(w_dt, ((0, 0), (0, LANES - heads)))], axis=1)
+    w_steps = jnp.pad(w_dt, ((0, 0), (0, LANES - heads)))
     bias = jnp.pad(dt_bias, (0, LANES - heads))[None]
     rate = jnp.pad(rates, (0, LANES - heads))[None]
 
-    xp, gate, bc, raw, halo = project(tokens, w_x, w_z, w_small)
+    xp, gate, bc, raw, halo = project(tokens, w_x, w_z, w_bc, w_steps)
     inside, c_vecs, opf, opb, sf, sb, dec, tot, totdec = local_part(
         xp, bc, halo, raw, bias, rate, aux, seg_rows, conv_x, conv_bc, heads
     )
     ent = exchange(tot, totdec, heads)
-    gated, sq = finish(inside, c_vecs, opf, opb, gate, sf, sb, dec, ent, heads)
-    squares = lax.psum(sq, "mp")
-    scale = lax.rsqrt(squares / (inner * mp_count) + 1e-05)
-    return (gated * scale * norm_gain).astype(BF16)
+    return finish(inside, c_vecs, opf, opb, gate, sf, sb, dec, ent, norm_gain, heads)
 
 
 def solution(mesh):

time: 230 us -> 204 us (0.89)
  blocking collectives: 20.3 us -> 0 us
  other arithmetic: 10.9 us -> 0.85 us
  local copies, waits for them, and re-layouts: 5.11 us -> 11 us
    psum x1 -> x0, blocking collectives: 20.3 us -> none  [shards(): squares = lax.psum(sq, 'mp')]
    convert_element_type x1 -> x0, other arithmetic: 6.15 us -> none  [shards(): return (gated * scale * norm_gain).astype(BF16)]
    pallas_call x1, Pallas kernels: 47.1 us -> 41.7 us  [exchange(): pl.pallas_call(functools.partial(exchange_kernel, heads, zs), in_specs=[v...]
    unnamed x15 -> x14, local copies, waits for them, and re-layouts: 1.7 us -> 6.48 us
    concatenate x1 -> x0, other arithmetic: 3.72 us -> none  [shards(): jnp.concatenate([w_bc, jnp.pad(w_dt, ((0, 0), (0, LANES - heads)))], axis=1)]
    pallas_call x1, Pallas kernels: 15.5 us -> 19 us  [finish(): pl.pallas_call(functools.partial(finish_kernel, heads, mp), grid=(blocks,...]
  transfers between devices with their start and end apart: 2 -> 2, of which waited for: 0 -> 0; matrix products, arithmetic and copies ran while one was open for 3% -> 2% of each run, Pallas kernels for 45% -> 51%
where the time goes in v2:
time: 204 us; the launch traced here: 203 us
  Pallas kernels  185 us (91%)
  local copies, waits for them, and re-layouts  11 us (5%)
  starting transfers between devices  4.85 us (2%)
    pallas_call x1, Pallas kernels, project(): pl.pallas_call(functools.partial(project_kernel, mp, seqs), in_specs=[any...  104 us
    pallas_call x1, Pallas kernels, exchange(): pl.pallas_call(functools.partial(exchange_kernel, heads, zs), in_specs=[v...  41.7 us
    pallas_call x1, Pallas kernels, local_part(): pl.pallas_call(functools.partial(local_kernel, heads), grid=(blocks,), in...  20.5 us
    pallas_call x1, Pallas kernels, finish(): pl.pallas_call(functools.partial(finish_kernel, heads, mp), grid=(blocks,...  19 us
    unnamed x14, local copies, waits for them, and re-layouts  6.48 us
  transfers between devices with their start and end apart: 2, of which 0 were waited for; matrix products, arithmetic and copies ran while one was open for 2% of the time, Pallas kernels for 51%

profile of v2, /device:TPU:0, one launch (start us, length us, event | category | flops | bytes accessed | tf_op | source)
XLA Modules:
  0.0 203.2 jit_solution(14808612320059057087)
XLA Ops:
  0.0 0.7 convert_element_type.5
  0.7 0.0 copy-start
  0.7 0.6 fusion.1
  1.3 1.3 collective-permute-start.1
  2.6 3.6 %collective-permute-start = (f32[1]{0:T(128)}, f32[1]{0:T(128)}, u32[]{:S(2)}, u32[]{:S(2)}) collective-permute-start(f32[1]{0:T(128)} %get-tuple-element.43), channel_id=1, source_target_pairs={{0,2},{2,4},{4,6},{6,8},{8,10},{10,12},{12,14},{14,16},{16,18},{18... | collective-permute-start | bytes 20 | tf_op jit(solution)/shard_map/ppermute | solution.py:745
  6.2 0.1 slice.31
  6.3 0.1 slice.30
  6.4 0.1 fusion
  6.4 0.1 broadcast_bitcast_fusion.1
  6.5 0.1 broadcast_bitcast_fusion
  6.6 1.4 copy.22
  8.0 1.3 pad_bitcast_fusion
  9.2 1.2 pad.11.wdt_ref
  10.4 0.0 copy-start.1
  10.4 103.8 %gather_and_project.1 = (bf16[1024,2048]{1,0:T(8,128)(2,1)}, bf16[1024,2048]{1,0:T(8,128)(2,1)}, bf16[1024,256]{1,0:T(8,128)(2,1)}, f32[1024,128]{1,0:T(8,128)}, bf16[2,16,2304]{2,1,0:T(8,128)(2,1)}) custom-call(bf16[1024,2048]{1,0:T(8,128)(2,1)} %tok_ref.1, bf16[4096,2048]{1,0:T(8,128)(2,1)} %wx_ref.1, bf16[4096,2048]{1,0:T(8,128)(2,1)} %wz_ref.1, ...), custom_call_target="tpu_custom_call" | custom-call | flops 37580963840 | bytes 36700160 | tf_op jit(solution)/shard_map/gather_and_project/pallas_call | solution.py:212
  114.2 0.0 collective-permute-done.1
  114.9 0.0 copy-done.1
  114.9 0.1 compare_convert_fusion.4
  114.9 0.1 slice.29
  115.0 0.1 broadcast_bitcast_fusion.2
  115.1 0.0 collective-permute-done
  115.8 0.1 compare_convert_fusion.5
  115.8 0.1 slice.28
  115.9 0.1 broadcast_bitcast_fusion.3
  116.0 0.0 copy-done
  116.0 0.1 stack.56
  116.1 1.0 copy.23.aux_ref
  117.1 20.5 %local_part.1 = (f32[1024,2048]{1,0:T(8,128)}, bf16[1024,128]{1,0:T(8,128)(2,1)}, f32[1024,128]{1,0:T(8,128)}, f32[1024,128]{1,0:T(8,128)}, f32[4,128,2048]{2,1,...) custom-call(bf16[1024,2048]{1,0:T(8,128)(2,1)} %get-tuple-element.19, ...), custom_call_target="tpu_custom_call" | custom-call | flops 2147483648 | bytes 20971520 | tf_op jit(solution)/shard_map/local_part/pallas_call | solution.py:355
  137.6 41.7 %exchange_states.1.ent_ref = bf16[4,2,32,2048]{3,2,1,0:T(8,128)(2,1)} custom-call(bf16[4,2,32,2048]{3,2,1,0:T(8,128)(2,1)} %get-tuple-element.31.tot_ref, f32[8,128]{1,0:T(8,128)} %get-tuple-element.32.dec_ref), custom_call_target="tpu_custom_call" | custom-call | flops 10485760 | bytes 4194304 | tf_op jit(solution)/shard_map/exchange_states/pallas_call | solution.py:595
  179.4 19.0 %finish.1 = bf16[1024,2048]{1,0:T(8,128)(2,1)} custom-call(f32[1024,2048]{1,0:T(8,128)} %get-tuple-element.23.inside_ref, bf16[1024,128]{1,0:T(8,128)(2,1)} %get-tuple-element.24.c_ref, f32[1024,128]{1,0:T(8,128)} %get-tuple-element.25.opf_ref, f32[1024,128]{1,0:T(8,128)} %get-tuple-element.26.opb_ref, bf16[1024,2048]{1,0:T(8,128)(2,1)} %get-tuple-element.27.gate_ref, ...), custom_call_target="tpu_custom_call" | custom-call | flops 1073741824 | bytes 20971520 | tf_op jit(solution)/shard_map/finish/pallas_call | solution.py:706
  198.4 4.8 %copy.29 = bf16[1024,2048]{1,0:T(8,128)(2,1)} copy(bf16[1024,2048]{1,0:T(8,128)(2,1)} %finish.1) | data formatting | bytes 8388608
  (5 shorter events, 0.0 us)
Async XLA Ops:
  0.7 115.3 %copy-start = (f32[1024]{0:T(1024)}, f32[1024]{0:T(1024)S(1)}, u32[]{:S(2)}) copy-start(f32[1024]{0:T(1024)S(1)} %convert_element_type.5) | copy-start | bytes 12292
  1.3 112.9 %collective-permute-start.1 = (f32[1]{0:T(128)}, f32[1]{0:T(128)}, u32[]{:S(2)}, u32[]{:S(2)}) collective-permute-start(f32[1]{0:T(128)} %get-tuple-element.42), channel_id=1, source_target_pairs={{2,0},{4,2},{6,4},{8,6},{10,8},{12,10},{14,12},{16,14},{18,16},{20... | collective-permute-start | bytes 20 | tf_op jit(solution)/shard_map/ppermute | solution.py:746
  2.6 112.5 %collective-permute-start = (f32[1]{0:T(128)}, f32[1]{0:T(128)}, u32[]{:S(2)}, u32[]{:S(2)}) collective-permute-start(f32[1]{0:T(128)} %get-tuple-element.43), channel_id=1, source_target_pairs={{0,2},{2,4},{4,6},{6,8},{8,10},{10,12},{12,14},{14,16},{16,18},{18... | collective-permute-start | bytes 20 | tf_op jit(solution)/shard_map/ppermute | solution.py:745
  10.4 104.4 %copy-start.1 = (s32[1024]{0:T(1024)S(1)}, s32[1024]{0:T(1024)}, u32[]{:S(2)}) copy-start(s32[1024]{0:T(1024)} %param.12) | copy-start | bytes 12292

commit v3 on v2

--- a/solution.py
+++ b/solution.py
@@ -21,9 +21,9 @@
 
 
 def project_kernel(
-    mp, seqs, tok_ref, wx_ref, wz_ref, wbc_ref, wdt_ref,
+    mp, seqs, tok_ref, wx_ref, wz_ref, wbc_ref, wdt_ref, seg_ref,
     xp_ref, gate_ref, bc_ref, raw_ref, halo_ref,
-    tok_v, wx_v, wz_v, ws_v, acc_x, acc_z, acc_s, stage_x, stage_z, edges, landed,
+    tok_v, wx_v, wz_v, wbc_v, wdt_v, acc_x, acc_z, acc_s, stage_x, stage_z, edges, landed,
     own_sem, w_sem, send_sem, recv_sem, out_sem, edge_s, edge_r,
 ):
     me = lax.axis_index("mp")
@@ -40,8 +40,8 @@
         for n, (src, dst) in enumerate(
             (
                 (wx_ref, wx_v),
-                (wbc_ref, ws_v.at[:, :2 * LANES]),
-                (wdt_ref, ws_v.at[:, 2 * LANES:]),
+                (wbc_ref, wbc_v),
+                (wdt_ref, wdt_v),
                 (wz_ref, wz_v),
             )
         )
@@ -62,23 +62,30 @@
     loads[0].start()
     pl.semaphore_wait(barrier, mp - 1 + 2)
 
+    def half(c, part):
+        return pl.ds(c * BLOCK + part * (BLOCK // 2), BLOCK // 2)
+
     def sends(c):
         return [
             pltpu.make_async_remote_copy(
-                src_ref=tok_ref.at[rows(c)], dst_ref=tok_v.at[me, rows(c)],
-                send_sem=send_sem.at[k, c], recv_sem=recv_sem.at[k, c],
+                src_ref=tok_ref.at[half(c, part)], dst_ref=tok_v.at[me, half(c, part)],
+                send_sem=send_sem.at[k, c, part], recv_sem=recv_sem.at[k, c, part],
                 device_id={"mp": lax.rem(me + k, mp)}, device_id_type=MESH,
             )
+            for part in range(2)
             for k in range(1, mp)
         ]
 
     def arrival(c, k):
         source = lax.rem(me - k + mp, mp)
-        return source, pltpu.make_async_remote_copy(
-            src_ref=tok_ref.at[rows(c)], dst_ref=tok_v.at[source, rows(c)],
-            send_sem=send_sem.at[k, c], recv_sem=recv_sem.at[k, c],
-            device_id={"mp": source}, device_id_type=MESH,
-        )
+        return source, [
+            pltpu.make_async_remote_copy(
+                src_ref=tok_ref.at[half(c, part)], dst_ref=tok_v.at[source, half(c, part)],
+                send_sem=send_sem.at[k, c, part], recv_sem=recv_sem.at[k, c, part],
+                device_id={"mp": source}, device_id_type=MESH,
+            )
+            for part in range(2)
+        ]
 
     def edge(way, to):
         return pltpu.make_async_remote_copy(
@@ -121,7 +128,16 @@
 
         def contract_small(source, first):
             depth = pl.ds(pl.multiple_of(source * width, width), width)
-            part = jnp.dot(tok_v[source, rows(c), :], ws_v[depth, :], preferred_element_type=F32)
+            piece = tok_v[source, rows(c), :]
+            part = jnp.concatenate(
+                [
+                    jnp.dot(piece, wbc_v[depth, :], preferred_element_type=F32),
+                    lax.dot_general(
+                        piece, wdt_v[:, depth], (((1,), (1,)), ((), ())), preferred_element_type=F32
+                    ),
+                ],
+                axis=1,
+            )
             acc_s[...] = part if first else acc_s[...] + part
 
         owns[c].wait()
@@ -135,19 +151,20 @@
         if n == 0:
             loads[3].wait()
         contract(me, wz_v, acc_z, stage_z, True, False)
-        for copy in going:
+        coming = sends(order[n + 1]) if n + 1 < chunks else []
+        for at_copy, copy in enumerate(going):
             copy.wait_send()
-        if n + 1 < chunks:
-            going = sends(order[n + 1])
-            for copy in going:
-                copy.start()
+            if coming:
+                coming[at_copy].start()
+        going = coming
         if n >= 2:
             for which in range(2):
                 out(order[n - 2], slot, which).wait()
         sources = []
         for k in range(1, mp):
-            source, copy = arrival(c, k)
-            copy.wait_recv()
+            source, copies = arrival(c, k)
+            for copy in copies:
+                copy.wait_recv()
             sources.append(source)
             contract(source, wx_v, acc_x, stage_x, False, k == mp - 1)
             contract_small(source, False)
@@ -156,11 +173,13 @@
         raw_ref[rows(c), :] = acc_s[:, 2 * LANES:]
         inner = stage_x.shape[2]
         if n == 0:
+            edges[0, :, inner + 2 * LANES:] = seg_ref[0]
             edges[0, :, :inner] = stage_x[slot, :16, :]
-            edges[0, :, inner:] = acc_s[:16, :2 * LANES].astype(BF16)
+            edges[0, :, inner:inner + 2 * LANES] = acc_s[:16, :2 * LANES].astype(BF16)
         if n == 1:
+            edges[1, :, inner + 2 * LANES:] = seg_ref[1]
             edges[1, :, :inner] = stage_x[slot, BLOCK - 16:, :]
-            edges[1, :, inner:] = acc_s[BLOCK - 16:, :2 * LANES].astype(BF16)
+            edges[1, :, inner:inner + 2 * LANES] = acc_s[BLOCK - 16:, :2 * LANES].astype(BF16)
 
             @pl.when(at > 0)
             def _():
@@ -183,6 +202,7 @@
     @pl.when(at == 0)
     def _():
         halo_ref[0] = jnp.zeros(halo_ref.shape[1:], BF16)
+        halo_ref[0, :, halo_ref.shape[2] - LANES:] = jnp.full((16, LANES), -1.0, BF16)
 
     @pl.when(at < seqs - 1)
     def _():
@@ -193,13 +213,14 @@
     @pl.when(at == seqs - 1)
     def _():
         halo_ref[1] = jnp.zeros(halo_ref.shape[1:], BF16)
+        halo_ref[1, :, halo_ref.shape[2] - LANES:] = jnp.full((16, LANES), -1.0, BF16)
 
     for n in range(max(0, chunks - 2), chunks):
         for which in range(2):
             out(order[n], n % 2, which).wait()
 
 
-def project(tokens, w_x, w_z, w_bc, w_steps):
+def project(tokens, w_x, w_z, w_bc, w_steps, seg_edges):
     tok, width = tokens.shape
     inner = w_x.shape[1]
     mp = lax.axis_size("mp")
@@ -208,31 +229,32 @@
     dma = pltpu.SemaphoreType.DMA
     anywhere = pl.BlockSpec(memory_space=pl.ANY)
     vmem = pl.BlockSpec(memory_space=pltpu.VMEM)
-    small = w_bc.shape[1] + w_steps.shape[1]
+    small = w_bc.shape[1] + w_steps.shape[0]
     return pl.pallas_call(
         functools.partial(project_kernel, mp, seqs),
-        in_specs=[anywhere] * 5,
+        in_specs=[anywhere] * 5 + [vmem],
         out_specs=[anywhere, anywhere, vmem, vmem, vmem],
         out_shape=[
             jax.ShapeDtypeStruct((tok, inner), BF16),
             jax.ShapeDtypeStruct((tok, inner), BF16),
             jax.ShapeDtypeStruct((tok, 2 * LANES), BF16),
             jax.ShapeDtypeStruct((tok, small - 2 * LANES), F32),
-            jax.ShapeDtypeStruct((2, 16, inner + 2 * LANES), BF16),
+            jax.ShapeDtypeStruct((2, 16, inner + 3 * LANES), BF16),
         ],
         scratch_shapes=[
             pltpu.VMEM((mp, tok, width), BF16),
             pltpu.VMEM(w_x.shape, BF16),
             pltpu.VMEM(w_z.shape, BF16),
-            pltpu.VMEM((w_x.shape[0], small), BF16),
+            pltpu.VMEM(w_bc.shape, BF16),
+            pltpu.VMEM(w_steps.shape, BF16),
             pltpu.VMEM((BLOCK, inner), F32),
             pltpu.VMEM((BLOCK, inner), F32),
             pltpu.VMEM((BLOCK, small), F32),
             pltpu.VMEM((2, BLOCK, inner), BF16),
             pltpu.VMEM((2, BLOCK, inner), BF16),
-            pltpu.VMEM((2, 16, inner + 2 * LANES), BF16),
-            pltpu.VMEM((2, 16, inner + 2 * LANES), BF16),
-            dma((chunks,)), dma((4,)), dma((mp, chunks)), dma((mp, chunks)), dma((2, 2)),
+            pltpu.VMEM((2, 16, inner + 3 * LANES), BF16),
+            pltpu.VMEM((2, 16, inner + 3 * LANES), BF16),
+            dma((chunks,)), dma((4,)), dma((mp, chunks, 2)), dma((mp, chunks, 2)), dma((2, 2)),
             dma((2,)), dma((2,)),
         ],
         compiler_params=pltpu.CompilerParams(
@@ -243,7 +265,7 @@
             bytes_accessed=width * mp * (2 * inner + small) * 2, transcendentals=0,
         ),
         name="gather_and_project",
-    )(tokens, w_x, w_z, w_bc, w_steps)
+    )(tokens, w_x, w_z, w_bc, w_steps, seg_edges)
 
 
 def silu(v):
@@ -362,7 +384,7 @@
             pl.BlockSpec((16, inner), right),
             pl.BlockSpec((16, 2 * LANES), left),
             pl.BlockSpec((16, 2 * LANES), right),
-            pl.BlockSpec((2, 16, inner + 2 * LANES), lambda b: (0, 0, 0)),
+            pl.BlockSpec((2, 16, inner + 3 * LANES), lambda b: (0, 0, 0)),
             pl.BlockSpec((BLOCK, LANES), row),
             pl.BlockSpec((1, LANES), fixed),
             pl.BlockSpec((1, LANES), fixed),
@@ -740,25 +762,22 @@
     )(inside, c_vecs, opf, opb, gate, sf, sb, dec, dec, ent, gain[None])
 
 
-def neighbours(rows):
-    count = lax.axis_size("seq")
-    from_left = lax.ppermute(rows[-1:], "seq", [(i, i + 1) for i in range(count - 1)])
-    from_right = lax.ppermute(rows[:1], "seq", [(i + 1, i) for i in range(count - 1)])
-    return from_left, from_right
-
-
 def shards(tokens, segment_ids, w_x, w_z, w_bc, w_dt, dt_bias, rates, conv_x, conv_bc, norm_gain):
     tok = tokens.shape[0]
     inner = w_x.shape[1]
     heads = w_dt.shape[1]
-    seq_count = lax.axis_size("seq")
-    position = lax.axis_index("seq")
     blocks = tok // BLOCK
 
     seg = segment_ids.astype(F32)
-    seg_left, seg_right = neighbours(seg)
-    seg_left = jnp.where(position > 0, seg_left, -1.0)
-    seg_right = jnp.where(position < seq_count - 1, seg_right, -1.0)
+    w_steps = jnp.pad(w_dt.T, ((0, LANES - heads), (0, 0)))
+    bias = jnp.pad(dt_bias, (0, LANES - heads))[None]
+    rate = jnp.pad(rates, (0, LANES - heads))[None]
+
+    seg_edges = jnp.stack([seg[0], seg[-1]]).astype(BF16)[:, None, None]
+    seg_edges = jnp.broadcast_to(seg_edges, (2, 16, LANES))
+    xp, gate, bc, raw, halo = project(tokens, w_x, w_z, w_bc, w_steps, seg_edges)
+    seg_left = halo[0, 15, inner + 2 * LANES:][:1].astype(F32)
+    seg_right = halo[1, 0, inner + 2 * LANES:][:1].astype(F32)
     before = jnp.concatenate([seg_left, seg[:-1]])
     after = jnp.concatenate([seg[1:], seg_right])
     by_block = lambda v: jnp.repeat(v, BLOCK)
@@ -776,11 +795,6 @@
         axis=1,
     )
     seg_rows = seg.reshape(blocks, 1, BLOCK)
-    w_steps = jnp.pad(w_dt, ((0, 0), (0, LANES - heads)))
-    bias = jnp.pad(dt_bias, (0, LANES - heads))[None]
-    rate = jnp.pad(rates, (0, LANES - heads))[None]
-
-    xp, gate, bc, raw, halo = project(tokens, w_x, w_z, w_bc, w_steps)
     inside, c_vecs, opf, opb, sf, sb, dec, tot, totdec = local_part(
         xp, bc, halo, raw, bias, rate, aux, seg_rows, conv_x, conv_bc, heads
     )

time: 204 us -> 201 us (0.985)
  starting transfers between devices: 4.85 us -> 0 us
    ppermute x2 -> x0, starting transfers between devices: 4.85 us -> none  [the longest x1 3.57 us: neighbours(): lax.ppermute(rows[-1:], 'seq', [(i, i + 1) for i in range(count - 1)])]
    unnamed x14 -> x13, local copies, waits for them, and re-layouts: 6.48 us -> 5.11 us
  transfers between devices with their start and end apart: 2 -> 0, of which waited for: 0 -> 0; matrix products, arithmetic and copies ran while one was open for 2% -> 0% of each run, Pallas kernels for 51% -> 0%
where the time goes in v3:
time: 201 us; the launch traced here: 200 us
  Pallas kernels  185 us (92%)
  local copies, waits for them, and re-layouts  12.3 us (6%)
  other arithmetic  2.19 us (1%)
    pallas_call x1, Pallas kernels, project(): pl.pallas_call(functools.partial(project_kernel, mp, seqs), in_specs=[any...  105 us
    pallas_call x1, Pallas kernels, exchange(): pl.pallas_call(functools.partial(exchange_kernel, heads, zs), in_specs=[v...  39.9 us
    pallas_call x1, Pallas kernels, local_part(): pl.pallas_call(functools.partial(local_kernel, heads), grid=(blocks,), in...  20.5 us
    pallas_call x1, Pallas kernels, finish(): pl.pallas_call(functools.partial(finish_kernel, heads, mp), grid=(blocks,...  18.9 us
    unnamed x13, local copies, waits for them, and re-layouts  5.11 us

profile of v3, /device:TPU:0, one launch (start us, length us, event | category | flops | bytes accessed | tf_op | source)
XLA Modules:
  0.0 200.3 jit_solution(13776683287048691184)
XLA Ops:
  0.0 1.3 pad_bitcast_fusion
  1.3 0.7 fusion.2
  1.9 0.0 copy-start
  1.9 0.6 fusion.3
  2.6 1.3 pad_maximum_fusion.2
  3.9 0.1 slice.47
  4.0 0.1 slice.46
  4.1 0.1 broadcast_bitcast_fusion.1
  4.2 0.1 broadcast_bitcast_fusion
  4.3 0.7 broadcast_in_dim.27.seg_ref
  4.9 0.1 fusion.1
  5.0 2.0 pad.11.wdt_ref
  7.0 0.0 copy-start.1
  7.0 105.2 %gather_and_project.1 = (bf16[1024,2048]{1,0:T(8,128)(2,1)}, bf16[1024,2048]{1,0:T(8,128)(2,1)}, bf16[1024,256]{1,0:T(8,128)(2,1)}, f32[1024,128]{1,0:T(8,128)}, bf16[2,16,2432]{2,1,0:T(8,128)(2,1)}) custom-call(bf16[1024,2048]{1,0:T(8,128)(2,1)} %tok_ref.1, bf16[4096,2048]{1,0:T(8,128)(2,1)} %wx_ref.1, bf16[4096,2048]{1,0:T(8,128)(2,1)} %wz_ref.1, ...), custom_call_target="tpu_custom_call" | custom-call | flops 37580963840 | bytes 36700160 | tf_op jit(solution)/shard_map/gather_and_project/pallas_call | solution.py:233
  112.2 1.2 fusion
  114.6 0.0 copy-done.1
  114.6 0.1 compare_convert_fusion.4
  114.6 0.1 slice.45
  114.7 0.1 broadcast_bitcast_fusion.2
  114.8 0.1 compare_convert_fusion.5
  114.9 0.1 slice.44
  115.0 0.1 broadcast_bitcast_fusion.3
  115.1 0.0 copy-done
  115.1 0.1 stack.60
  115.1 1.0 copy.20.aux_ref
  116.1 20.5 %local_part.1 = (f32[1024,2048]{1,0:T(8,128)}, bf16[1024,128]{1,0:T(8,128)(2,1)}, f32[1024,128]{1,0:T(8,128)}, f32[1024,128]{1,0:T(8,128)}, f32[4,128,2048]{2,1,...) custom-call(bf16[1024,2048]{1,0:T(8,128)(2,1)} %get-tuple-element.19, ...), custom_call_target="tpu_custom_call" | custom-call | flops 2147483648 | bytes 20971520 | tf_op jit(solution)/shard_map/local_part/pallas_call | solution.py:377
  136.7 39.9 %exchange_states.1.ent_ref = bf16[4,2,32,2048]{3,2,1,0:T(8,128)(2,1)} custom-call(bf16[4,2,32,2048]{3,2,1,0:T(8,128)(2,1)} %get-tuple-element.31.tot_ref, f32[8,128]{1,0:T(8,128)} %get-tuple-element.32.dec_ref), custom_call_target="tpu_custom_call" | custom-call | flops 10485760 | bytes 4194304 | tf_op jit(solution)/shard_map/exchange_states/pallas_call | solution.py:617
  176.6 18.9 %finish.1 = bf16[1024,2048]{1,0:T(8,128)(2,1)} custom-call(f32[1024,2048]{1,0:T(8,128)} %get-tuple-element.23.inside_ref, bf16[1024,128]{1,0:T(8,128)(2,1)} %get-tuple-element.24.c_ref, f32[1024,128]{1,0:T(8,128)} %get-tuple-element.25.opf_ref, f32[1024,128]{1,0:T(8,128)} %get-tuple-element.26.opb_ref, bf16[1024,2048]{1,0:T(8,128)(2,1)} %get-tuple-element.27.gate_ref, ...), custom_call_target="tpu_custom_call" | custom-call | flops 1073741824 | bytes 20971520 | tf_op jit(solution)/shard_map/finish/pallas_call | solution.py:728
  195.5 4.8 %copy.26 = bf16[1024,2048]{1,0:T(8,128)(2,1)} copy(bf16[1024,2048]{1,0:T(8,128)(2,1)} %finish.1) | data formatting | bytes 8388608
  (5 shorter events, 0.0 us)
Async XLA Ops:
  1.9 113.1 %copy-start = (f32[1024]{0:T(1024)}, f32[1024]{0:T(1024)S(1)}, u32[]{:S(2)}) copy-start(f32[1024]{0:T(1024)S(1)} %get-tuple-element.44) | copy-start | bytes 12292
  7.0 107.6 %copy-start.1 = (s32[1024]{0:T(1024)S(1)}, s32[1024]{0:T(1024)}, u32[]{:S(2)}) copy-start(s32[1024]{0:T(1024)} %param.12) | copy-start | bytes 12292
